TPU v7x, 768 devices: a whole 4x8x12 slice. The times are simulated.
768 devices in a mesh: lat: 192 (over z, y, core), lev: 4 (over x).
Axes of the slice: x: 4, y: 8, z: 12, core: 2. Of those that a mesh axis runs over, the one named last changes fastest.
Arguments:
- spectral_in: bfloat16 [4, 192, 4, 1280], P('lev', 'lat'), may hold values from -0.25 to 0.25
- legendre: bfloat16 [4, 192, 640, 384], P('lev', 'lat'), may hold values from -0.25 to 0.25
- slot_wave: int32 [4, 192], replicated, may hold values from 0 to 640, as said below
- row_length: int32 [384], P('lat'), may hold values from 16 to 2688, as said below
- quad_weight: float32 [384], replicated, may hold values from 8 to 64
Outputs:
- grid_field: bfloat16 [4, 384, 2688], P('lev', 'lat')
- spectral_out: bfloat16 [4, 192, 4, 1280], P('lev', 'lat')
Inputs may be any that keep to these rules, and one draw needn't show every extreme that they name: `slot_wave`: each wavenumber 0 to 639 stands in exactly one slot; all other slots hold 640. Each device holds at most 1 of the wavenumbers. `row_length`: lengths are multiples of 4; the two middle rows have length 2688.
All inputs are finite; a program needn't handle non-finite values.
Results may differ from a plain program's by a relative error of at most 0.0072.
Values may be sent and summed in bfloat16 or wider, within the bound.
No kernel may reach another device: no remote copies, remote signals or barrier semaphores. Data moves between devices by JAX's collectives and lax.ppermute only.
A program may use at most 32 MiB of HBM per device.

v0:
```python
import math

import jax
import jax.numpy as jnp
from jax import lax
from jax.sharding import PartitionSpec as P

M = 640
NLON = 2688


def transform_row(coeffs_row, length, wave_ids):
    lon_index = jnp.arange(NLON, dtype=jnp.int32)
    phase_turn = wave_ids[:, None] * lon_index[None, :] % length
    step_angle = 2.0 * math.pi / length.astype(jnp.float32)
    angles = phase_turn.astype(jnp.float32) * step_angle
    inside = (lon_index[None, :] < length) & (wave_ids[:, None] < M)
    dft_table = jnp.concatenate(
        [jnp.where(inside, jnp.cos(angles), 0.0), jnp.where(inside, jnp.sin(angles), 0.0)], 0
    ).astype(jnp.bfloat16)
    factor = jnp.where(wave_ids == 0, 1.0, 2.0).astype(jnp.bfloat16)
    stacked = jnp.concatenate(
        [coeffs_row[:, :, 0] * factor[:, None], -(coeffs_row[:, :, 1] * factor[:, None])], 0
    )
    grid_raw = jnp.dot(stacked.T, dft_table, preferred_element_type=jnp.float32)
    shaped = (grid_raw * (1.0 + 0.5 * jnp.tanh(grid_raw))).astype(jnp.bfloat16)
    summed = jnp.dot(shaped, dft_table.T, preferred_element_type=jnp.float32)
    slot_count = wave_ids.shape[0]
    length_float = length.astype(jnp.float32)
    real_back = summed[:, :slot_count] / length_float
    imag_back = -summed[:, slot_count:] / length_float
    four_row = jnp.stack([real_back, imag_back], -1).astype(jnp.bfloat16)
    return (shaped, jnp.transpose(four_row, (1, 0, 2)))


def transpose_lat(blocks):
    lat_index = lax.axis_index("lat")
    return lax.dynamic_index_in_dim(
        lax.all_gather(blocks[None], "lat", axis=0, tiled=True), lat_index, 1, keepdims=False
    )


def shards(spectral_in, legendre, slot_wave, row_length, quad_weight):
    lat_count = lax.axis_size("lat")
    lat_index = lax.axis_index("lat")
    lev_index = lax.axis_index("lev")
    own_lat = spectral_in.shape[1]
    fields = spectral_in.shape[2]
    degrees = legendre.shape[2]
    lat_total = legendre.shape[3]
    lat_local = row_length.shape[0]
    all_waves = slot_wave.reshape(-1)
    my_waves = lax.dynamic_slice(slot_wave, (lev_index, lat_index * own_lat), (1, own_lat)).reshape(
        own_lat
    )
    keep_mask = (jnp.arange(degrees, dtype=jnp.int32)[None, :] >= my_waves[:, None]).astype(
        jnp.bfloat16
    )
    coeffs = spectral_in.reshape(own_lat, fields, 2, degrees) * keep_mask[:, None, None, :]
    coeffs = coeffs.reshape(own_lat, fields * 2, degrees)
    matrices = legendre.reshape(own_lat, degrees, lat_total)
    fourier = jnp.einsum(
        "sqn,snl->lsq", coeffs, matrices, preferred_element_type=jnp.float32
    ).astype(jnp.bfloat16)
    blocks = fourier.reshape(lat_count, lat_local * own_lat * fields * 2)
    arrived = transpose_lat(blocks)
    row_major = jnp.transpose(
        arrived.reshape(lat_count, lat_local, own_lat, fields, 2), (1, 0, 2, 3, 4)
    )
    row_major = row_major.reshape(lat_local, lat_count * own_lat, fields, 2)
    spread = lax.all_to_all(row_major, "lev", split_axis=2, concat_axis=1, tiled=True)

    def one_row(packed):
        return transform_row(packed[0], packed[1], all_waves)

    shaped_rows, four_rows = lax.map(one_row, (spread, row_length))
    grid_field = jnp.transpose(shaped_rows, (1, 0, 2))
    regrouped = lax.all_to_all(four_rows, "lev", split_axis=1, concat_axis=2, tiled=True)
    outgoing = jnp.transpose(
        regrouped.reshape(lat_local, lat_count, own_lat * fields * 2), (1, 0, 2)
    )
    outgoing = outgoing.reshape(lat_count, lat_local * own_lat * fields * 2)
    returned = transpose_lat(outgoing)
    columns = returned.reshape(lat_total, own_lat, fields * 2)
    weighted = (columns * quad_weight[:, None, None]).astype(jnp.bfloat16)
    result = jnp.einsum("lsq,snl->sqn", weighted, matrices, preferred_element_type=jnp.float32)
    result = result * keep_mask[:, None, :].astype(jnp.float32)
    spectral_out = result.reshape(1, own_lat, fields, 2 * degrees).astype(jnp.bfloat16)
    return (grid_field, spectral_out)


def solution(mesh):
    in_specs = (P("lev", "lat", None, None), P("lev", "lat", None, None), P(), P("lat"), P())
    out_specs = (P("lev", "lat", None), P("lev", "lat", None, None))
    return jax.shard_map(shards, mesh=mesh, in_specs=in_specs, out_specs=out_specs, check_vma=False)
```

profile of v0, /device:TPU:1, one launch (start us, length us, event | category | flops | bytes accessed | tf_op | source)
XLA Modules:
  0.0 511.5 jit_solution(4957710564065305406)
XLA Ops:
  7.2 1.4 dynamic_slice.18
  8.6 0.7 fusion.29
  9.3 0.7 broadcast_multiply_fusion
  10.5 0.7 copy.37
  11.2 120.1 %all-gather.3.cloned.1.call-done = bf16[192,192,16]{1,2,0:T(8,128)(2,1)} async-done(((bf16[1,192,16]{1,2,0:T(8,128)(2,1)}), bf16[192,192,16]{1,2,0:T(8,128)(2,1)}) %all-gather.3.cloned.1.call-update) | async-done | bytes 1179664 | tf_op jit(solution)/shard_map/all_gather | solution.py:39
  131.3 1.4 constant_dynamic-slice_fusion
  132.7 0.7 copy.38
  133.5 0.6 copy.39
  134.1 4.0 all-to-all-start
  138.0 0.8 broadcast_in_dim_reshape.12
  138.8 0.8 reshape.260
  139.6 2.6 all-to-all-done
  142.3 240.5 %while.13 = (s32[]{:T(128)}, bf16[2,1,2688]{2,0,1:T(2,128)(2,1)S(1)}, bf16[2,768,1,2]{1,3,2,0:T(2,128)(2,1)S(1)}, bf16[2,768,1,2]{1,3,2,0:T(2,128)(2,1)S(1)}, s3...) while((s32[]{:T(128)}, ...), condition=%wide.wide.region_1.2_spmd, body=%wide.wide.region_0.1_spmd.sunk | while | flops 80549768 | bytes 24896456 | solution.py:76
  142.3 1.2 dynamic_slice.29
  145.5 0.7 iota_compare_fusion.4
  146.2 112.1 %fusion.47 = (bf16[768,2688]{1,0:T(8,128)(2,1)S(1)}, bf16[768,2688]{1,0:T(8,128)(2,1)S(1)}) fusion(f32[]{:T(128)S(6)} %div.33, s32[]{:T(128)S(6)} %select_n.70, s32[768]{0:T(1024)S(1)} %get-tuple-element.214, pred[]{:T(512)S(6)} %lt.69, pred[2688]{0:T(1024)(128)(4,1)S(1)} %iota_compare_fusion.4, pred[768]{0:T(1024)(128)(4,1)S(1)} %broadcast_compare_fusion.3), kind=kLoop, calls=%fused_computation.3.clone.clone.1 | loop fusion | flops 30965760 | bytes 8264073 | tf_op jit(solution)/shard_map/convert.4
  258.3 1.5 fusion.48
  259.9 2.5 fusion.49
  262.6 1.2 dynamic_slice.29
  265.8 0.7 iota_compare_fusion.4
  266.5 112.1 %fusion.47 = (bf16[768,2688]{1,0:T(8,128)(2,1)S(1)}, bf16[768,2688]{1,0:T(8,128)(2,1)S(1)}) fusion(f32[]{:T(128)S(6)} %div.33, s32[]{:T(128)S(6)} %select_n.70, s32[768]{0:T(1024)S(1)} %get-tuple-element.214, pred[]{:T(512)S(6)} %lt.69, pred[2688]{0:T(1024)(128)(4,1)S(1)} %iota_compare_fusion.4, pred[768]{0:T(1024)(128)(4,1)S(1)} %broadcast_compare_fusion.3), kind=kLoop, calls=%fused_computation.3.clone.clone.1 | loop fusion | flops 30965760 | bytes 8264073 | tf_op jit(solution)/shard_map/convert.4
  378.6 1.5 fusion.48
  380.2 2.5 fusion.49
  383.3 0.4 reshape.271
  383.7 6.5 %all_to_all.33 = bf16[4,2,384]{2,1,0:T(2,128)(2,1)S(1)} all-to-all(bf16[4,2,384]{2,1,0:T(2,128)(2,1)S(1)} %reshape.271), channel_id=1, replica_groups=mesh['lat'=192,'lev'=4] {'lev'}, dimensions={0} | all-to-all | bytes 12288 | tf_op jit(solution)/shard_map/all_to_all | solution.py:78
  390.2 0.8 reshape.272
  391.0 0.4 copy.46
  391.5 0.6 copy.51
  392.1 0.7 fusion.30
  392.8 109.0 %all-gather.5.cloned.1.call-done = bf16[192,192,16]{1,2,0:T(8,128)(2,1)} async-done(((bf16[1,192,16]{1,2,0:T(8,128)(2,1)}), bf16[192,192,16]{1,2,0:T(8,128)(2,1)}) %all-gather.5.cloned.1.call-update) | async-done | bytes 1179664 | tf_op jit(solution)/shard_map/all_gather | solution.py:39
  501.8 1.8 convert_reduce_fusion
  504.1 0.6 convert_element_type.134
  (45 shorter events, 1.9 us)
Async XLA Ops:
  7.2 2.9 copy-start
  7.2 124.1 %all-gather.3.cloned.1.call-start = ((), (), s32[]{:S(2)}) async-start(), calls=%async_computation.2 | async-start | bytes 1581056 | tf_op jit(solution)/shard_map/all_gather | solution.py:39
  134.1 8.1 %all-to-all-start = ((bf16[2,192,4,2]{1,3,0,2:T(2,128)(2,1)}), bf16[2,192,4,2]{1,3,0,2:T(2,128)(2,1)S(1)}, u32[]{:S(2)}, u32[]{:S(2)}) async-start(bf16[2,192,4,2]{1,3,0,2:T(2,128)(2,1)} %copy.39), calls=%async_computation | async-start | bytes 16384 | tf_op jit(solution)/shard_map/all_to_all | solution.py:71
  138.0 363.7 %all-gather.5.cloned.1.call-start = ((), (), s32[]{:S(2)}) async-start(), calls=%async_computation.3 | async-start | bytes 1581056 | tf_op jit(solution)/shard_map/all_gather | solution.py:39
  142.3 361.4 %copy-start.1 = (f32[384]{0:T(512)S(1)}, f32[384]{0:T(512)}, u32[]{:S(2)}) copy-start(f32[384]{0:T(512)} %param.11) | copy-start | bytes 4612
  382.8 121.9 %copy-start.2 = (bf16[2,1,2688]{2,0,1:T(2,128)(2,1)}, bf16[2,1,2688]{2,0,1:T(2,128)(2,1)S(1)}, u32[]{:S(2)}) copy-start(bf16[2,1,2688]{2,0,1:T(2,128)(2,1)S(1)} %get-tuple-element.40) | copy-start | bytes 32260
Sparse Core Ops, SparseCore 0:
  12.3 118.9 all-gather.2
  392.2 109.4 all-gather.4
where the time goes:
time: 512 us
  waiting for transfers between devices  232 us (45%)
  other arithmetic  229 us (45%)
  between operations  14.2 us (3%)
  local copies, waits for them, and re-layouts  13 us (3%)
  matrix products  8.49 us (2%)
  blocking collectives  6.49 us (1%)
    all_gather x2, waiting for transfers between devices, transpose_lat(): lax.all_gather(blocks[None], 'lat', axis=0, tiled=True)  229 us
    another operation x2, other arithmetic  224 us
  transfers between devices with their start and end apart: 3, of which 3 were waited for; matrix products, arithmetic and copies ran while one was open for 0% of the time, Pallas kernels for 0%

commit v1 on v0

v1 whole, which is shorter than its diff:
```python
import math

import jax
import jax.numpy as jnp
from jax import lax
from jax.experimental import pallas as pl
from jax.experimental.pallas import tpu as pltpu
from jax.sharding import Mesh
from jax.sharding import PartitionSpec as P

M = 640
NDEG = 640
NLAT = 384
NLON = 2688
SLOTS = 768
ZC = 24
YX = 32
NB = 128
NA = 21
NA_PAD = 24

F32 = jnp.float32
BF16 = jnp.bfloat16


def iota(shape, dim):
    return lax.broadcasted_iota(jnp.int32, shape, dim)


def dot(x, y, dims=((1,), (0,))):
    return lax.dot_general(x, y, (dims, ((), ())), preferred_element_type=F32)


def one_hot(cond):
    return jnp.where(cond, 1.0, 0.0).astype(BF16)


def row_selector():
    l = iota((NLAT, 128), 0)
    return one_hot((((l >> 2) & 7) * 2 + (l & 1)) == (iota((NLAT, 128), 1) & 15))


def row_target():
    l = iota((ZC, NLAT), 1)
    return ((l >> 5) * 2 + ((l >> 1) & 1)) == iota((ZC, NLAT), 0)


def pair_selector():
    p = iota((128, 128), 0)
    target = ((p >> 6) * 4 + (p & 3)) * 16 + ((p >> 2) & 7) * 2 + ((p >> 5) & 1)
    return one_hot(iota((128, 128), 1) == target)


def by24(l):
    return (l * 2731) >> 16


def slot_selector():
    l = iota((128, SLOTS), 1)
    return one_hot((iota((128, SLOTS), 0) & 31) == (l - by24(l) * ZC))


def legendre_in(spec, leg, wave):
    both = jnp.concatenate([spec[:, :NDEG].astype(F32), spec[:, NDEG:].astype(F32)], 0)
    kept = jnp.where(iota(both.shape, 1) >= wave, both, 0.0).astype(BF16)
    four = dot(kept, leg).astype(BF16).astype(F32)
    mine = row_target()
    spread = jnp.concatenate([jnp.where(mine, four[q : q + 1], 0.0) for q in range(8)], 0)
    moved = dot(spread.astype(BF16), row_selector())
    group = iota((ZC, 128), 1) >> 4
    out = jnp.zeros((ZC, 128), F32)
    for q in range(8):
        out = jnp.where(group == q, moved[q * ZC : (q + 1) * ZC], out)
    return out


def turn_in(got):
    padded = jnp.concatenate([got, jnp.zeros((32 - ZC, 128), F32)], 0)
    moved = dot(pair_selector(), jnp.concatenate([padded] * 4, 0).astype(BF16), ((1,), (1,)))
    group = iota((YX, 128), 1) >> 5
    out = jnp.zeros((YX, 128), F32)
    for q in range(4):
        out = jnp.where(group == q, moved[q * YX : (q + 1) * YX], out)
    return out


def spread_groups(x, count, width):
    group = iota(x.shape, 1) >> width
    return jnp.concatenate([jnp.where(group == q, x, 0.0) for q in range(count)], 0).astype(BF16)


def turn_out(got):
    moved = dot(spread_groups(got, 4, 5), pair_selector(), ((0,), (0,)))
    total = moved[:32] + moved[32:64] + moved[64:96] + moved[96:]
    return total[:ZC]


def legendre_out(got, leg, wave):
    moved = dot(spread_groups(got, 8, 4), row_selector(), ((1,), (1,)))
    mine = row_target()
    rows = [
        jnp.sum(jnp.where(mine, moved[q * ZC : (q + 1) * ZC], 0.0), 0, keepdims=True)
        for q in range(8)
    ]
    weighted = jnp.concatenate(rows, 0).astype(BF16)
    result = dot(weighted, leg, ((1,), (1,)))
    result = jnp.where(iota(result.shape, 1) >= wave, result, 0.0)
    return result[:4], result[4:]


def slot_order(waves):
    l = iota((192, SLOTS), 1)
    i = by24(l)
    j = l - i * ZC
    pick = one_hot(iota((192, SLOTS), 0) == (((j >> 1) * 8 + (i >> 2)) * 2 + (j & 1)))
    parts = jnp.concatenate([(waves >> 3).astype(F32), (waves & 7).astype(F32)], 0).astype(BF16)
    got = dot(parts, pick)
    full = got[:4] * 8.0 + got[4:]
    lane = iota((4, SLOTS), 1)
    return jnp.sum(jnp.where((by24(lane) & 3) == iota((4, SLOTS), 0), full, 0.0), 0, keepdims=True)


SIN_TERMS = [(-1.0) ** n * math.pi ** (2 * n + 1) / math.factorial(2 * n + 1) for n in range(7)]
COS_TERMS = [(-1.0) ** n * math.pi ** (2 * n) / math.factorial(2 * n) for n in range(8)]


def circle(points, waves, length):
    product = points * waves
    inverse = 1.0 / length
    rest = product - jnp.floor(product * inverse + 0.5) * length
    turn = rest * inverse
    square = turn * turn
    sine = jnp.full_like(square, SIN_TERMS[-1])
    for term in SIN_TERMS[-2::-1]:
        sine = sine * square + term
    sine = sine * turn
    cosine = jnp.full_like(square, COS_TERMS[-1])
    for term in COS_TERMS[-2::-1]:
        cosine = cosine * square + term
    return 1.0 - 2.0 * sine * sine, 2.0 * sine * cosine


def split(x):
    high = x.astype(BF16)
    return high, (x - high.astype(F32)).astype(BF16)


def table_a(waves, length):
    points = iota((NA_PAD, SLOTS), 0).astype(F32) * float(NB)
    cosine, sine = circle(points, waves, length)
    both = jnp.concatenate([cosine, sine], 1)
    high, low = split(both)
    return jnp.concatenate([high.astype(F32), low.astype(F32)], 0).astype(BF16)


def table_b(waves, length):
    return circle(iota((NB, waves.shape[1]), 0).astype(F32), waves, length)


def gather_slots(got):
    moved = dot(spread_groups(got, 4, 5), slot_selector())
    own = by24(iota((YX, SLOTS), 1)) == iota((YX, SLOTS), 0)
    return [
        jnp.sum(jnp.where(own, moved[q * YX : (q + 1) * YX], 0.0), 0, keepdims=True)
        for q in range(4)
    ]


def grid_row(real, imag, waves, length, weight, outer, cosine, sine):
    factor = jnp.where(waves >= float(M), 0.0, jnp.where(waves == 0.0, 1.0, 2.0))
    real = real * factor
    imag = imag * factor
    mixed = jnp.concatenate([real * cosine - imag * sine, -(real * sine + imag * cosine)], 1)
    high, low = split(mixed)
    raw = dot(outer, high, ((1,), (1,)))
    raw = raw[:NA_PAD] + raw[NA_PAD:] + dot(outer[:NA_PAD], low, ((1,), (1,)))
    shaped = raw * (1.0 + 0.5 * jnp.tanh(raw))
    point = iota((NA_PAD, NB), 0) * NB + iota((NA_PAD, NB), 1)
    shaped = jnp.where(point.astype(F32) < length, shaped, 0.0)
    rounded = shaped.astype(BF16).astype(F32)
    twice = jnp.concatenate([rounded, rounded], 0).astype(BF16)
    back = dot(twice, outer, ((0,), (0,)))
    back_cos, back_sin = back[:, :SLOTS], back[:, SLOTS:]
    live = jnp.where(waves >= float(M), 0.0, 1.0) / length
    out_real = jnp.sum(back_cos * cosine - back_sin * sine, 0, keepdims=True) * live
    out_imag = -jnp.sum(back_cos * sine + back_sin * cosine, 0, keepdims=True) * live
    out = [(v.astype(BF16).astype(F32) * weight).astype(BF16).astype(F32) for v in (out_real, out_imag)]
    return rounded, out[0], out[1]


def scatter_slots(rows):
    own = by24(iota((YX, SLOTS), 1)) == iota((YX, SLOTS), 0)
    spread = jnp.concatenate([jnp.where(own, row, 0.0) for row in rows], 0).astype(BF16)
    moved = dot(spread, slot_selector(), ((1,), (1,)))
    group = iota((YX, 128), 1) >> 5
    out = jnp.zeros((YX, 128), F32)
    for q in range(4):
        out = jnp.where(group == q, moved[q * YX : (q + 1) * YX], out)
    return out


def my_wave(place_ref, waves_ref):
    return waves_ref[place_ref[0], place_ref[1]]


def legendre_in_kernel(place_ref, waves_ref, spec_ref, leg_ref, out_ref):
    out = legendre_in(spec_ref[0, 0], leg_ref[0, 0], my_wave(place_ref, waves_ref))
    out_ref[...] = out.reshape(ZC, 1, 128)


def turn_in_kernel(got_ref, out_ref):
    out_ref[...] = turn_in(got_ref[...].reshape(ZC, 128)).reshape(YX, 1, 128)


def tables_kernel(length_ref, waves_ref, order_ref, outer_ref, cos_ref, sin_ref):
    waves = slot_order(waves_ref[...])
    order_ref[...] = waves
    for r in range(2):
        length = length_ref[r].astype(F32)
        outer_ref[r] = table_a(waves, length)
        for part in range(SLOTS // 128):
            lanes = slice(part * 128, (part + 1) * 128)
            cosine, sine = table_b(waves[:, lanes], length)
            cos_ref[r, :, lanes] = cosine
            sin_ref[r, :, lanes] = sine


def grid_kernel(
    place_ref, length_ref, weight_ref, got_ref, order_ref, outer_ref, cos_ref, sin_ref, grid_ref, out_ref
):
    rows = gather_slots(got_ref[...].reshape(YX, 128))
    done = []
    for r in range(2):
        done.append(
            grid_row(
                rows[r],
                rows[2 + r],
                order_ref[...],
                length_ref[r].astype(F32),
                weight_ref[2 * place_ref[1] + r],
                outer_ref[r],
                cos_ref[r],
                sin_ref[r],
            )
        )
    for a in range(NA):
        pair = jnp.concatenate([done[0][0][a : a + 1], done[1][0][a : a + 1]], 0)
        grid_ref[0, :, a * NB : (a + 1) * NB] = pair.astype(BF16)
    out = scatter_slots([done[0][1], done[1][1], done[0][2], done[1][2]])
    out_ref[...] = out.reshape(YX, 1, 128)


def turn_out_kernel(got_ref, out_ref):
    out_ref[...] = turn_out(got_ref[...].reshape(YX, 128)).reshape(ZC, 1, 128)


def legendre_out_kernel(place_ref, waves_ref, got_ref, leg_ref, out_ref):
    real, imag = legendre_out(
        got_ref[...].reshape(ZC, 128), leg_ref[0, 0], my_wave(place_ref, waves_ref)
    )
    out_ref[0, 0, :, :NDEG] = real.astype(BF16)
    out_ref[0, 0, :, NDEG:] = imag.astype(BF16)


VMEM = pl.BlockSpec(memory_space=pltpu.VMEM)
SMEM = pl.BlockSpec(memory_space=pltpu.SMEM)


def call(kernel, name, in_specs, outs, cost):
    single = not isinstance(outs, list)
    return pl.pallas_call(
        kernel,
        name=name,
        in_specs=in_specs,
        out_specs=VMEM if single else [VMEM] * len(outs),
        out_shape=outs if single else tuple(outs),
        compiler_params=pltpu.CompilerParams(vmem_limit_bytes=24 * 1024 * 1024),
        cost_estimate=pl.CostEstimate(flops=cost, bytes_accessed=100000, transcendentals=0),
    )


def shape(*dims, dtype=F32):
    return jax.ShapeDtypeStruct(dims, dtype)


def shards(spectral_in, legendre, slot_wave, row_length, quad_weight):
    lat_index = (lax.axis_index("z") * 8 + lax.axis_index("y")) * 2 + lax.axis_index("c")
    place = jnp.stack([lax.axis_index("x"), lat_index]).astype(jnp.int32)
    to_send = call(legendre_in_kernel, "legendre_in", [SMEM, SMEM, VMEM, VMEM], shape(ZC, 1, 128), 10**6)(
        place, slot_wave, spectral_in, legendre
    )
    got = lax.all_to_all(to_send, ("z", "c"), 0, 0, tiled=True)
    to_send = call(turn_in_kernel, "turn_in", [VMEM], shape(YX, 1, 128), 10**6)(got)
    got = lax.all_to_all(to_send, ("y", "x"), 0, 0, tiled=True)
    order, outer, cosine, sine = call(
        tables_kernel,
        "tables",
        [SMEM, VMEM],
        [
            shape(1, SLOTS),
            shape(2, 2 * NA_PAD, 2 * SLOTS, dtype=BF16),
            shape(2, NB, SLOTS),
            shape(2, NB, SLOTS),
        ],
        10**9,
    )(row_length, slot_wave)
    grid_field, to_send = call(
        grid_kernel,
        "grid",
        [SMEM, SMEM, SMEM, VMEM, VMEM, VMEM, VMEM, VMEM],
        [shape(1, 2, NLON, dtype=BF16), shape(YX, 1, 128)],
        10**6,
    )(place, row_length, quad_weight, got, order, outer, cosine, sine)
    got = lax.all_to_all(to_send, ("y", "x"), 0, 0, tiled=True)
    to_send = call(turn_out_kernel, "turn_out", [VMEM], shape(ZC, 1, 128), 10**6)(got)
    got = lax.all_to_all(to_send, ("z", "c"), 0, 0, tiled=True)
    spectral_out = call(
        legendre_out_kernel, "legendre_out", [SMEM, SMEM, VMEM, VMEM], shape(1, 1, 4, 2 * NDEG, dtype=BF16), 10**6
    )(place, slot_wave, got, legendre)
    return grid_field, spectral_out


def solution(mesh):
    cut = Mesh(mesh.devices.reshape(12, 8, 2, 4), ("z", "y", "c", "x"))
    lat = ("z", "y", "c")
    in_specs = (P("x", lat, None, None), P("x", lat, None, None), P(), P(lat), P())
    out_specs = (P("x", lat, None), P("x", lat, None, None))
    return jax.shard_map(shards, mesh=cut, in_specs=in_specs, out_specs=out_specs, check_vma=False)
```

time: 512 us -> 80.9 us (0.16)
  other arithmetic: 229 us -> 0.08 us
  waiting for transfers between devices: 232 us -> 6.63 us
  blocking collectives: 6.49 us -> 52.7 us
  between operations: 14.2 us -> 0.71 us
  local copies, waits for them, and re-layouts: 13 us -> 2.32 us
  matrix products: 8.49 us -> 0 us
  Pallas kernels: 0 us -> 8.21 us
  starting transfers between devices: 4.01 us -> 9.8 us
    all_gather x2 -> x0, waiting for transfers between devices: 229 us -> none  [transpose_lat(): lax.all_gather(blocks[None], 'lat', axis=0, tiled=True)]
    another operation x4 -> x1, other arithmetic: 224 us -> 0.08 us  [shards(): place = jnp.stack([lax.axis_index('x'), lat_index]).astype(jnp.int32)]
    all_to_all x1 -> x3, blocking collectives: 6.49 us -> 52.7 us  [the longest x2 41.2 us: shards(): got = lax.all_to_all(to_send, ('z', 'c'), 0, 0, tiled=True)]
    dot_general x6 -> x0, matrix products: 8.49 us -> none  [the longest x2 4.96 us: transform_row(): summed = jnp.dot(shaped, dft_table.T, preferred_element_type=jnp.float32)]
    pallas_call x0 -> x6, Pallas kernels: none -> 8.21 us  [the longest x1 2.69 us: shards(): call(grid_kernel, 'grid', [SMEM, SMEM, SMEM, VMEM, VMEM, VMEM, VMEM, VMEM...]
    dynamic_slice x5 -> x0, local copies, waits for them, and re-layouts: 5.98 us -> none  [the longest x2 2.49 us: shards(): shaped_rows, four_rows = lax.map(one_row, (spread, row_length))]
    all_to_all x1, starting transfers between devices: 3.97 us -> 9.8 us  [shards(): got = lax.all_to_all(to_send, ('y', 'x'), 0, 0, tiled=True)]
  transfers between devices with their start and end apart: 3 -> 1, of which waited for: 3 -> 1; matrix products, arithmetic and copies ran while one was open for 0% -> 0% of each run, Pallas kernels for 0% -> 2%
where the time goes in v1:
time: 80.9 us; the launch traced here: 80.5 us
  blocking collectives  52.7 us (65%)
  starting transfers between devices  9.8 us (12%)
  Pallas kernels  8.21 us (10%)
  waiting for transfers between devices  6.63 us (8%)
  local copies, waits for them, and re-layouts  2.32 us (3%)
    all_to_all x2, blocking collectives, shards(): got = lax.all_to_all(to_send, ('z', 'c'), 0, 0, tiled=True)  41.2 us
    all_to_all x1, blocking collectives, shards(): got = lax.all_to_all(to_send, ('y', 'x'), 0, 0, tiled=True)  11.5 us
    all_to_all x1, starting transfers between devices, shards(): got = lax.all_to_all(to_send, ('y', 'x'), 0, 0, tiled=True)  9.8 us
    all_to_all x1, waiting for transfers between devices, shards(): got = lax.all_to_all(to_send, ('y', 'x'), 0, 0, tiled=True)  6.63 us
    pallas_call x1, Pallas kernels, shards(): call(grid_kernel, 'grid', [SMEM, SMEM, SMEM, VMEM, VMEM, VMEM, VMEM, VMEM...  2.69 us
    unnamed x12, local copies, waits for them, and re-layouts  2.32 us
    pallas_call x1, Pallas kernels, shards(): call(tables_kernel, 'tables', [SMEM, VMEM], [shape(1, SLOTS), shape(2, 2...  1.94 us
    pallas_call x1, Pallas kernels, shards(): call(legendre_out_kernel, 'legendre_out', [SMEM, SMEM, VMEM, VMEM], shape...  1.63 us
  transfers between devices with their start and end apart: 1, of which 1 were waited for; matrix products, arithmetic and copies ran while one was open for 0% of the time, Pallas kernels for 2%

profile of v1, /device:TPU:1, one launch (start us, length us, event | category | flops | bytes accessed | tf_op | source)
XLA Modules:
  0.0 80.5 jit_solution(11874690793498410921)
XLA Ops:
  0.6 0.0 copy-start.3
  0.7 0.0 copy-start.2
  0.7 0.1 pad_add_fusion.place_ref
  0.7 0.6 copy-done.3
  1.3 0.0 copy-done.2
  1.3 0.0 copy-start
  1.3 1.0 %copy-done = bf16[1,1,640,384]{3,2,1,0:T(8,128)(2,1)S(1)} copy-done((bf16[1,1,640,384]{3,2,1,0:T(8,128)(2,1)S(1)}, bf16[1,1,640,384]{3,2,1,0:T(8,128)(2,1)}, u32[]{:S(2)}) %copy-start) | copy-done | bytes 491544
  2.4 1.0 %legendre_in.1 = f32[24,1,128]{2,1,0:T(1,128)S(1)} custom-call(s32[2]{0:T(128)S(1)} %pad_add_fusion.place_ref, s32[4,192]{1,0:T(4,128)S(1)} %copy-done.2, bf16[1,1,4,1280]{3,2,1,0:T(4,128)(2,1)S(1)} %copy-done.3, bf16[1,1,640,384]{3,2,1,0:T(8,128)(2,1)S(1)} %copy-done), custom_call_target="tpu_custom_call" | custom-call | flops 1000000 | bytes 100000 | tf_op jit(solution)/shard_map/legendre_in/pallas_call | solution.py:289
  3.4 25.9 %all_to_all.20.got_ref = f32[24,1,128]{2,1,0:T(1,128)S(1)} all-to-all(f32[24,1,128]{2,1,0:T(1,128)S(1)} %legendre_in.1), channel_id=1, replica_groups=mesh['z'=12,'y'=8,'c'=2,'x'=4] {'z','c'}, dimensions={0} | all-to-all | bytes 24576 | tf_op jit(solution)/shard_map/all_to_all | solution.py:292
  29.3 0.8 turn_in.1
  30.0 0.0 copy-start.5
  30.0 9.8 %all-to-all-start.1 = ((f32[32,1,128]{2,1,0:T(1,128)}), f32[32,1,128]{2,1,0:T(1,128)S(1)}, u32[]{:S(2)}, u32[]{:S(2)}) async-start(f32[32,1,128]{2,1,0:T(1,128)} %turn_in.1), calls=%async_computation.1 | async-start | bytes 32768 | tf_op jit(solution)/shard_map/all_to_all | solution.py:294
  39.8 0.0 copy-done.5
  39.9 1.9 %tables.1 = (f32[1,768]{1,0:T(1,128)S(1)}, bf16[2,48,1536]{2,1,0:T(8,128)(2,1)S(1)}, f32[2,128,768]{2,1,0:T(8,128)S(1)}, f32[2,128,768]{2,1,0:T(8,128)S(1)}) custom-call(s32[2]{0:T(128)S(1)} %copy-done.5, s32[4,192]{1,0:T(4,128)S(1)} %copy-done.2), custom_call_target="tpu_custom_call" | custom-call | flops 1000000000 | bytes 100000 | tf_op jit(solution)/shard_map/tables/pallas_call | solution.py:295
  41.8 6.6 %all-to-all-done.1.got_ref = f32[32,1,128]{2,1,0:T(1,128)S(1)} async-done(((f32[32,1,128]{2,1,0:T(1,128)}), f32[32,1,128]{2,1,0:T(1,128)S(1)}, u32[]{:S(2)}, u32[]{:S(2)}) %all-to-all-start.1) | async-done | bytes 16416 | tf_op jit(solution)/shard_map/all_to_all | solution.py:294
  48.4 0.0 copy-start.4
  48.4 0.7 copy-done.4
  49.1 0.0 copy-start.1
  49.1 2.7 %grid.1 = (bf16[1,2,2688]{2,1,0:T(2,128)(2,1)}, f32[32,1,128]{2,1,0:T(1,128)S(1)}) custom-call(s32[2]{0:T(128)S(1)} %pad_add_fusion.place_ref, s32[2]{0:T(128)S(1)} %copy-done.5, f32[384]{0:T(512)S(1)} %copy-done.4, f32[32,1,128]{2,1,0:T(1,128)S(1)} %all-to-all-done.1.got_ref, f32[1,768]{1,0:T(1,128)S(1)} %get-tuple-element.8.order_ref, ...), custom_call_target="tpu_custom_call" | custom-call | flops 1000000 | bytes 100000 | tf_op jit(solution)/shard_map/grid/pallas_call | solution.py:307
  51.8 11.5 %all_to_all.21.got_ref = f32[32,1,128]{2,1,0:T(1,128)S(1)} all-to-all(f32[32,1,128]{2,1,0:T(1,128)S(1)} %get-tuple-element.13), channel_id=1, replica_groups=mesh['z'=12,'y'=8,'c'=2,'x'=4] {'y','x'}, dimensions={0} | all-to-all | bytes 32768 | tf_op jit(solution)/shard_map/all_to_all | solution.py:314
  63.4 0.2 turn_out.1
  63.6 15.3 %all_to_all.22.got_ref = f32[24,1,128]{2,1,0:T(1,128)S(1)} all-to-all(f32[24,1,128]{2,1,0:T(1,128)S(1)} %turn_out.1), channel_id=1, replica_groups=mesh['z'=12,'y'=8,'c'=2,'x'=4] {'z','c'}, dimensions={0} | all-to-all | bytes 24576 | tf_op jit(solution)/shard_map/all_to_all | solution.py:316
  78.9 0.0 copy-done.1
  78.9 1.6 %legendre_out.1 = bf16[1,1,4,1280]{3,2,1,0:T(4,128)(2,1)} custom-call(s32[2]{0:T(128)S(1)} %pad_add_fusion.place_ref, s32[4,192]{1,0:T(4,128)S(1)} %copy-done.2, f32[24,1,128]{2,1,0:T(1,128)S(1)} %all_to_all.22.got_ref, bf16[1,1,640,384]{3,2,1,0:T(8,128)(2,1)S(1)} %copy-done.1), custom_call_target="tpu_custom_call" | custom-call | flops 1000000 | bytes 100000 | tf_op jit(solution)/shard_map/legendre_out/pallas_call | solution.py:317
Async XLA Ops:
  0.6 0.7 copy-start.3
  0.7 0.7 copy-start.2
  1.3 1.0 %copy-start = (bf16[1,1,640,384]{3,2,1,0:T(8,128)(2,1)S(1)}, bf16[1,1,640,384]{3,2,1,0:T(8,128)(2,1)}, u32[]{:S(2)}) copy-start(bf16[1,1,640,384]{3,2,1,0:T(8,128)(2,1)} %leg_ref.3) | copy-start | bytes 1474564
  30.0 9.8 %copy-start.5 = (s32[2]{0:T(128)S(1)}, s32[2]{0:T(128)}, u32[]{:S(2)}) copy-start(s32[2]{0:T(128)} %length_ref.3) | copy-start | bytes 28
  30.0 18.4 %all-to-all-start.1 = ((f32[32,1,128]{2,1,0:T(1,128)}), f32[32,1,128]{2,1,0:T(1,128)S(1)}, u32[]{:S(2)}, u32[]{:S(2)}) async-start(f32[32,1,128]{2,1,0:T(1,128)} %turn_in.1), calls=%async_computation.1 | async-start | bytes 32768 | tf_op jit(solution)/shard_map/all_to_all | solution.py:294
  48.4 0.7 copy-start.4
  49.1 29.7 %copy-start.1 = (bf16[1,1,640,384]{3,2,1,0:T(8,128)(2,1)S(1)}, bf16[1,1,640,384]{3,2,1,0:T(8,128)(2,1)}, u32[]{:S(2)}) copy-start(bf16[1,1,640,384]{3,2,1,0:T(8,128)(2,1)} %leg_ref.3) | copy-start | bytes 1474564

commit v2 on v1

--- a/solution.py
+++ b/solution.py
@@ -145,16 +145,13 @@
     return high, (x - high.astype(F32)).astype(BF16)
 
 
-def table_a(waves, length):
-    points = iota((NA_PAD, SLOTS), 0).astype(F32) * float(NB)
-    cosine, sine = circle(points, waves, length)
-    both = jnp.concatenate([cosine, sine], 1)
-    high, low = split(both)
-    return jnp.concatenate([high.astype(F32), low.astype(F32)], 0).astype(BF16)
-
-
-def table_b(waves, length):
-    return circle(iota((NB, waves.shape[1]), 0).astype(F32), waves, length)
+def tables(waves, length):
+    row = iota((48, SLOTS), 0)
+    points = jnp.where(row < NA_PAD, row * NB, jnp.where(row < 40, (row - NA_PAD) * 8, row - 40))
+    cosine, sine = circle(points.astype(F32), waves, length)
+    high, low = split(jnp.concatenate([cosine[:NA_PAD], sine[:NA_PAD]], 1))
+    outer = jnp.concatenate([high.astype(F32), low.astype(F32)], 0).astype(BF16)
+    return outer, cosine[NA_PAD:], sine[NA_PAD:]
 
 
 def gather_slots(got):
@@ -166,26 +163,46 @@
     ]
 
 
-def grid_row(real, imag, waves, length, weight, outer, cosine, sine):
-    factor = jnp.where(waves >= float(M), 0.0, jnp.where(waves == 0.0, 1.0, 2.0))
+def factors(waves, lengths, weights):
+    empty = waves >= float(M)
+    rows = [jnp.where(empty, 0.0, jnp.where(waves == 0.0, 1.0, 2.0))]
+    rows += [jnp.where(empty, 0.0, w / n) for n, w in zip(lengths, weights, strict=True)]
+    rows += [jnp.full_like(waves, n) for n in lengths]
+    return jnp.concatenate(rows + [jnp.zeros((3, SLOTS), F32)], 0)
+
+
+def grid_row(real, imag, factor, back_factor, length, outer, cosine, sine):
     real = real * factor
     imag = imag * factor
-    mixed = jnp.concatenate([real * cosine - imag * sine, -(real * sine + imag * cosine)], 1)
-    high, low = split(mixed)
+    cos_one, sin_one = cosine[16:], sine[16:]
+    start_real = real * cos_one - imag * sin_one
+    start_imag = real * sin_one + imag * cos_one
+    mixed = []
+    for j in range(16):
+        c, s = cosine[j : j + 1], sine[j : j + 1]
+        mixed.append(
+            jnp.concatenate([start_real * c - start_imag * s, -(start_real * s + start_imag * c)], 1)
+        )
+    high, low = split(jnp.concatenate(mixed, 0))
     raw = dot(outer, high, ((1,), (1,)))
     raw = raw[:NA_PAD] + raw[NA_PAD:] + dot(outer[:NA_PAD], low, ((1,), (1,)))
     shaped = raw * (1.0 + 0.5 * jnp.tanh(raw))
     point = iota((NA_PAD, NB), 0) * NB + iota((NA_PAD, NB), 1)
-    shaped = jnp.where(point.astype(F32) < length, shaped, 0.0)
+    shaped = jnp.where(point.astype(F32) < length[:, :NB], shaped, 0.0)
     rounded = shaped.astype(BF16).astype(F32)
     twice = jnp.concatenate([rounded, rounded], 0).astype(BF16)
     back = dot(twice, outer, ((0,), (0,)))
-    back_cos, back_sin = back[:, :SLOTS], back[:, SLOTS:]
-    live = jnp.where(waves >= float(M), 0.0, 1.0) / length
-    out_real = jnp.sum(back_cos * cosine - back_sin * sine, 0, keepdims=True) * live
-    out_imag = -jnp.sum(back_cos * sine + back_sin * cosine, 0, keepdims=True) * live
-    out = [(v.astype(BF16).astype(F32) * weight).astype(BF16).astype(F32) for v in (out_real, out_imag)]
-    return rounded, out[0], out[1]
+    total_cos = jnp.zeros((8, SLOTS), F32)
+    total_sin = jnp.zeros((8, SLOTS), F32)
+    for j in range(16):
+        c, s = cosine[j : j + 1], sine[j : j + 1]
+        rows = slice(j * 8, (j + 1) * 8)
+        back_cos, back_sin = back[rows, :SLOTS], back[rows, SLOTS:]
+        total_cos = total_cos + (back_cos * c - back_sin * s)
+        total_sin = total_sin + (back_cos * s + back_sin * c)
+    out_real = jnp.sum(total_cos * cos_one - total_sin * sin_one, 0, keepdims=True)
+    out_imag = -jnp.sum(total_cos * sin_one + total_sin * cos_one, 0, keepdims=True)
+    return rounded, out_real * back_factor, out_imag * back_factor
 
 
 def scatter_slots(rows):
@@ -199,35 +216,31 @@
     return out
 
 
-def my_wave(place_ref, waves_ref):
-    return waves_ref[place_ref[0], place_ref[1]]
-
-
-def legendre_in_kernel(place_ref, waves_ref, spec_ref, leg_ref, out_ref):
-    out = legendre_in(spec_ref[0, 0], leg_ref[0, 0], my_wave(place_ref, waves_ref))
-    out_ref[...] = out.reshape(ZC, 1, 128)
+def tables_kernel(
+    place_ref, waves_ref, length_ref, weight_ref, wave_ref, factor_ref, outer_ref, cos_ref, sin_ref
+):
+    waves = waves_ref[...]
+    here = (iota((4, 192), 0) == place_ref[0]) & (iota((4, 192), 1) == place_ref[1])
+    own = jnp.where(here, waves.astype(F32), 0.0)
+    own = jnp.sum(jnp.sum(own, 0, keepdims=True), 1, keepdims=True)
+    wave_ref[...] = jnp.broadcast_to(own, (1, 128))
+    order = slot_order(waves)
+    lengths = [length_ref[r].astype(F32) for r in range(2)]
+    factor_ref[...] = factors(order, lengths, [weight_ref[2 * place_ref[1] + r] for r in range(2)])
+    for r in range(2):
+        outer_ref[r], cos_ref[r], sin_ref[r] = tables(order, lengths[r])
+
+
+def legendre_in_kernel(wave_ref, spec_ref, leg_ref, out_ref):
+    wave = wave_ref[:, :1].astype(jnp.int32)
+    out_ref[...] = legendre_in(spec_ref[0, 0], leg_ref[0, 0], wave).reshape(ZC, 1, 128)
 
 
 def turn_in_kernel(got_ref, out_ref):
     out_ref[...] = turn_in(got_ref[...].reshape(ZC, 128)).reshape(YX, 1, 128)
 
 
-def tables_kernel(length_ref, waves_ref, order_ref, outer_ref, cos_ref, sin_ref):
-    waves = slot_order(waves_ref[...])
-    order_ref[...] = waves
-    for r in range(2):
-        length = length_ref[r].astype(F32)
-        outer_ref[r] = table_a(waves, length)
-        for part in range(SLOTS // 128):
-            lanes = slice(part * 128, (part + 1) * 128)
-            cosine, sine = table_b(waves[:, lanes], length)
-            cos_ref[r, :, lanes] = cosine
-            sin_ref[r, :, lanes] = sine
-
-
-def grid_kernel(
-    place_ref, length_ref, weight_ref, got_ref, order_ref, outer_ref, cos_ref, sin_ref, grid_ref, out_ref
-):
+def grid_kernel(got_ref, factor_ref, outer_ref, cos_ref, sin_ref, grid_ref, out_ref):
     rows = gather_slots(got_ref[...].reshape(YX, 128))
     done = []
     for r in range(2):
@@ -235,9 +248,9 @@
             grid_row(
                 rows[r],
                 rows[2 + r],
-                order_ref[...],
-                length_ref[r].astype(F32),
-                weight_ref[2 * place_ref[1] + r],
+                factor_ref[0:1],
+                factor_ref[1 + r : 2 + r],
+                factor_ref[3 + r : 4 + r],
                 outer_ref[r],
                 cos_ref[r],
                 sin_ref[r],
@@ -254,10 +267,9 @@
     out_ref[...] = turn_out(got_ref[...].reshape(YX, 128)).reshape(ZC, 1, 128)
 
 
-def legendre_out_kernel(place_ref, waves_ref, got_ref, leg_ref, out_ref):
-    real, imag = legendre_out(
-        got_ref[...].reshape(ZC, 128), leg_ref[0, 0], my_wave(place_ref, waves_ref)
-    )
+def legendre_out_kernel(wave_ref, got_ref, leg_ref, out_ref):
+    wave = wave_ref[:, :1].astype(jnp.int32)
+    real, imag = legendre_out(got_ref[...].reshape(ZC, 128), leg_ref[0, 0], wave)
     out_ref[0, 0, :, :NDEG] = real.astype(BF16)
     out_ref[0, 0, :, NDEG:] = imag.astype(BF16)
 
@@ -266,7 +278,7 @@
 SMEM = pl.BlockSpec(memory_space=pltpu.SMEM)
 
 
-def call(kernel, name, in_specs, outs, cost):
+def call(kernel, name, in_specs, outs, flops=10**6):
     single = not isinstance(outs, list)
     return pl.pallas_call(
         kernel,
@@ -275,7 +287,7 @@
         out_specs=VMEM if single else [VMEM] * len(outs),
         out_shape=outs if single else tuple(outs),
         compiler_params=pltpu.CompilerParams(vmem_limit_bytes=24 * 1024 * 1024),
-        cost_estimate=pl.CostEstimate(flops=cost, bytes_accessed=100000, transcendentals=0),
+        cost_estimate=pl.CostEstimate(flops=flops, bytes_accessed=100000, transcendentals=0),
     )
 
 
@@ -286,37 +298,34 @@
 def shards(spectral_in, legendre, slot_wave, row_length, quad_weight):
     lat_index = (lax.axis_index("z") * 8 + lax.axis_index("y")) * 2 + lax.axis_index("c")
     place = jnp.stack([lax.axis_index("x"), lat_index]).astype(jnp.int32)
-    to_send = call(legendre_in_kernel, "legendre_in", [SMEM, SMEM, VMEM, VMEM], shape(ZC, 1, 128), 10**6)(
-        place, slot_wave, spectral_in, legendre
+    wave, factor, outer, cosine, sine = call(
+        tables_kernel,
+        "tables",
+        [SMEM, VMEM, SMEM, SMEM],
+        [
+            shape(1, 128),
+            shape(8, SLOTS),
+            shape(2, 2 * NA_PAD, 2 * SLOTS, dtype=BF16),
+            shape(2, 24, SLOTS),
+            shape(2, 24, SLOTS),
+        ],
+        2 * 10**9,
+    )(place, slot_wave, row_length, quad_weight)
+    to_send = call(legendre_in_kernel, "legendre_in", [VMEM] * 3, shape(ZC, 1, 128))(
+        wave, spectral_in, legendre
     )
     got = lax.all_to_all(to_send, ("z", "c"), 0, 0, tiled=True)
-    to_send = call(turn_in_kernel, "turn_in", [VMEM], shape(YX, 1, 128), 10**6)(got)
+    to_send = call(turn_in_kernel, "turn_in", [VMEM], shape(YX, 1, 128))(got)
     got = lax.all_to_all(to_send, ("y", "x"), 0, 0, tiled=True)
-    order, outer, cosine, sine = call(
-        tables_kernel,
-        "tables",
-        [SMEM, VMEM],
-        [
-            shape(1, SLOTS),
-            shape(2, 2 * NA_PAD, 2 * SLOTS, dtype=BF16),
-            shape(2, NB, SLOTS),
-            shape(2, NB, SLOTS),
-        ],
-        10**9,
-    )(row_length, slot_wave)
     grid_field, to_send = call(
-        grid_kernel,
-        "grid",
-        [SMEM, SMEM, SMEM, VMEM, VMEM, VMEM, VMEM, VMEM],
-        [shape(1, 2, NLON, dtype=BF16), shape(YX, 1, 128)],
-        10**6,
-    )(place, row_length, quad_weight, got, order, outer, cosine, sine)
+        grid_kernel, "grid", [VMEM] * 5, [shape(1, 2, NLON, dtype=BF16), shape(YX, 1, 128)]
+    )(got, factor, outer, cosine, sine)
     got = lax.all_to_all(to_send, ("y", "x"), 0, 0, tiled=True)
-    to_send = call(turn_out_kernel, "turn_out", [VMEM], shape(ZC, 1, 128), 10**6)(got)
+    to_send = call(turn_out_kernel, "turn_out", [VMEM], shape(ZC, 1, 128))(got)
     got = lax.all_to_all(to_send, ("z", "c"), 0, 0, tiled=True)
     spectral_out = call(
-        legendre_out_kernel, "legendre_out", [SMEM, SMEM, VMEM, VMEM], shape(1, 1, 4, 2 * NDEG, dtype=BF16), 10**6
-    )(place, slot_wave, got, legendre)
+        legendre_out_kernel, "legendre_out", [VMEM] * 3, shape(1, 1, 4, 2 * NDEG, dtype=BF16)
+    )(wave, got, legendre)
     return grid_field, spectral_out
 
 

time: 80.9 us -> 77.9 us (0.963)
  blocking collectives: 52.7 us -> 71 us
  starting transfers between devices: 9.8 us -> 0 us
  waiting for transfers between devices: 6.63 us -> 0 us
  Pallas kernels: 8.21 us -> 5.21 us
  local copies, waits for them, and re-layouts: 2.32 us -> 0.61 us
    all_to_all x1 -> x2, blocking collectives: 11.5 us -> 29.6 us  [shards(): got = lax.all_to_all(to_send, ('y', 'x'), 0, 0, tiled=True)]
    all_to_all x1 -> x0, starting transfers between devices: 9.8 us -> none  [shards(): got = lax.all_to_all(to_send, ('y', 'x'), 0, 0, tiled=True)]
    all_to_all x1 -> x0, waiting for transfers between devices: 6.63 us -> none  [shards(): got = lax.all_to_all(to_send, ('y', 'x'), 0, 0, tiled=True)]
    pallas_call x6, Pallas kernels: 8.21 us -> 5.21 us  [the longest x1 2.22 us: shards(): call(grid_kernel, 'grid', [VMEM] * 5, [shape(1, 2, NLON, dtype=BF16), sha...]
    unnamed x12 -> x10, local copies, waits for them, and re-layouts: 2.32 us -> 0.61 us
  transfers between devices with their start and end apart: 1 -> 0, of which waited for: 1 -> 0; matrix products, arithmetic and copies ran while one was open for 0% -> 0% of each run, Pallas kernels for 2% -> 0%
where the time goes in v2:
time: 77.9 us; the launch traced here: 77.6 us
  blocking collectives  71 us (91%)
  Pallas kernels  5.21 us (7%)
    all_to_all x2, blocking collectives, shards(): got = lax.all_to_all(to_send, ('z', 'c'), 0, 0, tiled=True)  41.4 us
    all_to_all x2, blocking collectives, shards(): got = lax.all_to_all(to_send, ('y', 'x'), 0, 0, tiled=True)  29.6 us
    pallas_call x1, Pallas kernels, shards(): call(grid_kernel, 'grid', [VMEM] * 5, [shape(1, 2, NLON, dtype=BF16), sha...  2.22 us

profile of v2, /device:TPU:1, one launch (start us, length us, event | category | flops | bytes accessed | tf_op | source)
XLA Modules:
  0.0 77.6 jit_solution(8534459232856227654)
XLA Ops:
  0.6 0.0 copy-start.2
  0.7 0.0 copy-start.3
  0.7 0.0 copy-start.4
  0.7 0.1 pad_add_fusion.place_ref
  0.7 0.6 copy-done.2
  1.3 0.0 copy-done.3
  1.3 0.0 copy-done.4
  1.3 0.0 copy-start
  1.3 0.0 copy-start.1
  1.3 1.2 %tables.1 = (f32[1,128]{1,0:T(1,128)S(1)}, f32[8,768]{1,0:T(8,128)S(1)}, bf16[2,48,1536]{2,1,0:T(8,128)(2,1)S(1)}, f32[2,24,768]{2,1,0:T(8,128)S(1)}, f32[2,24,768]{2,1,0:T(8,128)S(1)}) custom-call(s32[2]{0:T(128)S(1)} %pad_add_fusion.place_ref, s32[4,192]{1,0:T(4,128)S(1)} %copy-done.2, s32[2]{0:T(128)S(1)} %copy-done.4, f32[384]{0:T(512)S(1)} %copy-done.3), custom_call_target="tpu_custom_call" | custom-call | flops 2000000000 | bytes 100000 | tf_op jit(solution)/shard_map/tables/pallas_call | solution.py:301
  2.5 0.0 copy-done
  2.5 0.0 copy-done.1
  2.5 0.4 legendre_in.1
  3.0 25.9 %all_to_all.20.got_ref = f32[24,1,128]{2,1,0:T(1,128)S(1)} all-to-all(f32[24,1,128]{2,1,0:T(1,128)S(1)} %legendre_in.1), channel_id=1, replica_groups=mesh['z'=12,'y'=8,'c'=2,'x'=4] {'z','c'}, dimensions={0} | all-to-all | bytes 24576 | tf_op jit(solution)/shard_map/all_to_all | solution.py:317
  28.9 0.2 turn_in.1
  29.1 18.1 %all_to_all.21.got_ref = f32[32,1,128]{2,1,0:T(1,128)S(1)} all-to-all(f32[32,1,128]{2,1,0:T(1,128)S(1)} %turn_in.1), channel_id=1, replica_groups=mesh['z'=12,'y'=8,'c'=2,'x'=4] {'y','x'}, dimensions={0} | all-to-all | bytes 32768 | tf_op jit(solution)/shard_map/all_to_all | solution.py:319
  47.1 2.2 %grid.1 = (bf16[1,2,2688]{2,1,0:T(2,128)(2,1)}, f32[32,1,128]{2,1,0:T(1,128)S(1)}) custom-call(f32[32,1,128]{2,1,0:T(1,128)S(1)} %all_to_all.21.got_ref, f32[8,768]{1,0:T(8,128)S(1)} %get-tuple-element.10.factor_ref, bf16[2,48,1536]{2,1,0:T(8,128)(2,1)S(1)} %get-tuple-element.11.outer_ref, f32[2,24,768]{2,1,0:T(8,128)S(1)} %get-tuple-element.12.cos_ref, ...), custom_call_target="tpu_custom_call" | custom-call | flops 1000000 | bytes 100000 | tf_op jit(solution)/shard_map/grid/pallas_call | solution.py:320
  49.3 11.5 %all_to_all.22.got_ref = f32[32,1,128]{2,1,0:T(1,128)S(1)} all-to-all(f32[32,1,128]{2,1,0:T(1,128)S(1)} %get-tuple-element.15), channel_id=1, replica_groups=mesh['z'=12,'y'=8,'c'=2,'x'=4] {'y','x'}, dimensions={0} | all-to-all | bytes 32768 | tf_op jit(solution)/shard_map/all_to_all | solution.py:323
  60.9 0.2 turn_out.1
  61.1 15.5 %all_to_all.23.got_ref = f32[24,1,128]{2,1,0:T(1,128)S(1)} all-to-all(f32[24,1,128]{2,1,0:T(1,128)S(1)} %turn_out.1), channel_id=1, replica_groups=mesh['z'=12,'y'=8,'c'=2,'x'=4] {'z','c'}, dimensions={0} | all-to-all | bytes 24576 | tf_op jit(solution)/shard_map/all_to_all | solution.py:325
  76.6 1.0 %legendre_out.1 = bf16[1,1,4,1280]{3,2,1,0:T(4,128)(2,1)} custom-call(f32[1,128]{1,0:T(1,128)S(1)} %get-tuple-element.9.wave_ref, f32[24,1,128]{2,1,0:T(1,128)S(1)} %all_to_all.23.got_ref, bf16[1,1,640,384]{3,2,1,0:T(8,128)(2,1)S(1)} %copy-done), custom_call_target="tpu_custom_call" | custom-call | flops 1000000 | bytes 100000 | tf_op jit(solution)/shard_map/legendre_out/pallas_call | solution.py:326
Async XLA Ops:
  0.6 0.7 copy-start.2
  0.7 0.7 copy-start.3
  0.7 0.7 copy-start.4
  1.3 1.2 %copy-start = (bf16[1,1,640,384]{3,2,1,0:T(8,128)(2,1)S(1)}, bf16[1,1,640,384]{3,2,1,0:T(8,128)(2,1)}, u32[]{:S(2)}) copy-start(bf16[1,1,640,384]{3,2,1,0:T(8,128)(2,1)} %leg_ref.3) | copy-start | bytes 1474564
  1.3 1.2 %copy-start.1 = (bf16[1,1,4,1280]{3,2,1,0:T(4,128)(2,1)S(1)}, bf16[1,1,4,1280]{3,2,1,0:T(4,128)(2,1)}, u32[]{:S(2)}) copy-start(bf16[1,1,4,1280]{3,2,1,0:T(4,128)(2,1)} %spec_ref.1) | copy-start | bytes 30724

commit v3 on v2

v3 whole, which is shorter than its diff:
```python
import math

import jax
import jax.numpy as jnp
from jax import lax
from jax.experimental import pallas as pl
from jax.experimental.pallas import tpu as pltpu
from jax.sharding import Mesh
from jax.sharding import PartitionSpec as P

M = 640
NDEG = 640
NLAT = 384
NLON = 2688
SLOTS = 768
ZC = 24
YX = 32
NB = 128
NA = 21
NA_PAD = 24
NT = 48

PARTS = [slice(q * 128, (q + 1) * 128) for q in range(6)]

F32 = jnp.float32
BF16 = jnp.bfloat16


def iota(shape, dim):
    return lax.broadcasted_iota(jnp.int32, shape, dim)


def dot(x, y, dims=((1,), (0,))):
    return lax.dot_general(x, y, (dims, ((), ())), preferred_element_type=F32)


def one_hot(cond):
    return jnp.where(cond, 1.0, 0.0).astype(BF16)


def row_selector():
    l = iota((NLAT, 128), 0)
    lane = iota((NLAT, 128), 1)
    return one_hot((lane & 63) == ((l & 1) * 32 + (l >> 5) * 2 + ((l >> 1) & 1)))


def legendre_in(spec, leg, wave):
    both = jnp.concatenate([spec[:, :NDEG].astype(F32), spec[:, NDEG:].astype(F32)], 0)
    kept = jnp.where(iota(both.shape, 1) >= wave, both, 0.0).astype(BF16)
    four = dot(kept, leg).astype(BF16).astype(F32)
    mine = ((iota((8, NLAT), 1) >> 2) & 7) == iota((8, NLAT), 0)
    spread = jnp.concatenate([jnp.where(mine, four[q : q + 1], 0.0) for q in range(8)], 0)
    moved = dot(spread.astype(BF16), row_selector())
    return jnp.where(iota((YX, 128), 1) < 64, moved[:YX], moved[YX:])


def legendre_out(got, weight, leg, wave):
    low = iota((YX, 128), 1) < 64
    spread = jnp.concatenate([jnp.where(low, got, 0.0), jnp.where(low, 0.0, got)], 0)
    moved = dot(spread.astype(BF16), row_selector(), ((1,), (1,)))
    mine = ((iota((8, NLAT), 1) >> 2) & 7) == iota((8, NLAT), 0)
    rows = [
        jnp.sum(jnp.where(mine, moved[q * 8 : (q + 1) * 8], 0.0), 0, keepdims=True) for q in range(8)
    ]
    weighted = (jnp.concatenate(rows, 0) * weight).astype(BF16)
    result = dot(weighted, leg, ((1,), (1,)))
    result = jnp.where(iota(result.shape, 1) >= wave, result, 0.0)
    return result[:4], result[4:]


def turn(got):
    flipped = jnp.concatenate([got] * 4, 0).T
    group = iota((32, 128), 1) >> 5
    out = flipped[:32]
    for q in range(1, 4):
        out = jnp.where(group == q, flipped[q * 32 : (q + 1) * 32], out)
    return out


def roll(x, shift, axis):
    return pltpu.roll(x, shift % x.shape[axis], axis)


def swap_fours(x):
    line = iota(x.shape, 0) & 3
    group = iota(x.shape, 1) >> 5
    out = x
    for d in range(1, 4):
        moved = roll(x, -32 * d, 1)
        out = jnp.where(line - group == d, roll(moved, d, 0), out)
        out = jnp.where(line - group == d - 4, roll(moved, d - 4, 0), out)
    return out


def slot_order(waves):
    k = iota((192, 128), 0) & 31
    lane = iota((192, 128), 1)
    pick = one_hot(k == ((lane >> 6) * 16 + (lane & 7) * 2 + ((lane >> 5) & 1)))
    both = jnp.concatenate([(waves >> 3).astype(F32), (waves & 7).astype(F32)], 0)
    part = iota((8, 192), 1) >> 5
    spread = jnp.concatenate([jnp.where(part == q, both, 0.0) for q in range(6)], 0)
    moved = dot(spread.astype(BF16), pick)
    row = iota((8, 128), 0)
    scale = jnp.where((row & 3) == ((iota((8, 128), 1) >> 3) & 3), jnp.where(row < 4, 8.0, 1.0), 0.0)
    return jnp.concatenate(
        [jnp.sum(moved[q * 8 : (q + 1) * 8] * scale, 0, keepdims=True) for q in range(6)], 1
    )


SIN_TERMS = [(-1.0) ** n * math.pi ** (2 * n + 1) / math.factorial(2 * n + 1) for n in range(7)]
COS_TERMS = [(-1.0) ** n * math.pi ** (2 * n) / math.factorial(2 * n) for n in range(8)]


def circle(points, waves, length):
    product = points * waves
    inverse = 1.0 / length
    rest = product - jnp.floor(product * inverse + 0.5) * length
    turn = rest * inverse
    square = turn * turn
    sine = jnp.full_like(square, SIN_TERMS[-1])
    for term in SIN_TERMS[-2::-1]:
        sine = sine * square + term
    sine = sine * turn
    cosine = jnp.full_like(square, COS_TERMS[-1])
    for term in COS_TERMS[-2::-1]:
        cosine = cosine * square + term
    return 1.0 - 2.0 * sine * sine, 2.0 * sine * cosine


def split(x):
    high = x.astype(BF16)
    return high, (x - high.astype(F32)).astype(BF16)


def tables(waves, length):
    row = iota((48, SLOTS), 0)
    points = jnp.where(row < NA_PAD, row * NB, jnp.where(row < 40, (row - NA_PAD) * 8, row - 40))
    cosine, sine = circle(points.astype(F32), waves, length)
    parts = []
    for lanes in PARTS:
        parts += [cosine[:NA_PAD, lanes], sine[:NA_PAD, lanes]]
    high, low = split(jnp.concatenate(parts, 1))
    outer = jnp.concatenate([high.astype(F32), low.astype(F32)], 0).astype(BF16)
    return outer, cosine[NA_PAD:], sine[NA_PAD:]


def factors(waves, lengths):
    empty = waves >= float(M)
    rows = [jnp.where(empty, 0.0, jnp.where(waves == 0.0, 1.0, 2.0))]
    rows += [jnp.where(empty, 0.0, 1.0 / n) for n in lengths]
    rows += [jnp.full_like(waves, n) for n in lengths]
    return jnp.concatenate(rows + [jnp.zeros((3, SLOTS), F32)], 0)


def grid_rows(got, factor, outer, cosine, sine):
    got = swap_fours(got)
    raws = [jnp.zeros((NB, NT), F32) for _ in range(2)]
    for q, lanes in enumerate(PARTS):
        for r in range(2):
            wide = slice(q * 256, (q + 1) * 256)
            cos_one, sin_one = cosine[r, 16:, lanes], sine[r, 16:, lanes]
            real = got[q * 4 + r : q * 4 + r + 1] * factor[0:1, lanes]
            imag = got[q * 4 + 2 + r : q * 4 + 3 + r] * factor[0:1, lanes]
            start_real = real * cos_one - imag * sin_one
            start_imag = real * sin_one + imag * cos_one
            mixed = []
            for j in range(16):
                c, s = cosine[r, j : j + 1, lanes], sine[r, j : j + 1, lanes]
                mixed.append(
                    jnp.concatenate([start_real * c - start_imag * s, -(start_real * s + start_imag * c)], 1)
                )
            high = jnp.concatenate(mixed, 0).astype(BF16)
            raws[r] = raws[r] + dot(high, outer[r, :, wide], ((1,), (1,)))
    grids, flips = [], []
    for r in range(2):
        raw = raws[r].T
        raw = raw[:NA_PAD] + raw[NA_PAD:]
        shaped = raw * (1.0 + 0.5 * jnp.tanh(raw))
        point = iota((NA_PAD, NB), 0) * NB + iota((NA_PAD, NB), 1)
        shaped = jnp.where(point.astype(F32) < factor[3 + r : 4 + r, :NB], shaped, 0.0)
        rounded = shaped.astype(BF16).astype(F32)
        grids.append(rounded)
        flips.append(jnp.concatenate([rounded, rounded], 0).T.astype(BF16))
    lines = [None] * 24
    for q, lanes in enumerate(PARTS):
        for r in range(2):
            wide = slice(q * 256, (q + 1) * 256)
            back = dot(flips[r], outer[r, :, wide])
            total_cos = jnp.zeros((8, 128), F32)
            total_sin = jnp.zeros((8, 128), F32)
            for j in range(16):
                c, s = cosine[r, j : j + 1, lanes], sine[r, j : j + 1, lanes]
                rows = slice(j * 8, (j + 1) * 8)
                back_cos, back_sin = back[rows, :128], back[rows, 128:]
                total_cos = total_cos + (back_cos * c - back_sin * s)
                total_sin = total_sin + (back_cos * s + back_sin * c)
            cos_one, sin_one = cosine[r, 16:, lanes], sine[r, 16:, lanes]
            part = factor[1 + r : 2 + r, lanes]
            lines[q * 4 + r] = jnp.sum(total_cos * cos_one - total_sin * sin_one, 0, keepdims=True) * part
            lines[q * 4 + 2 + r] = jnp.sum(total_cos * sin_one + total_sin * cos_one, 0, keepdims=True) * -part
    back = swap_fours(jnp.concatenate(lines, 0))
    return grids[0], grids[1], back.astype(BF16).astype(F32)


def tables_kernel(place_ref, waves_ref, wave_ref, factor_ref, outer_ref, cos_ref, sin_ref):
    waves = waves_ref[...]
    here = (iota((4, 192), 0) == place_ref[0]) & (iota((4, 192), 1) == place_ref[1])
    own = jnp.where(here, waves.astype(F32), 0.0)
    own = jnp.sum(jnp.sum(own, 0, keepdims=True), 1, keepdims=True)
    wave_ref[...] = jnp.broadcast_to(own, (1, 128))
    order = slot_order(waves)
    lengths = [place_ref[2 + r].astype(F32) for r in range(2)]
    factor_ref[...] = factors(order, lengths)
    for r in range(2):
        outer_ref[r], cos_ref[r], sin_ref[r] = tables(order, lengths[r])


def legendre_in_kernel(wave_ref, spec_ref, leg_ref, out_ref):
    wave = wave_ref[:, :1].astype(jnp.int32)
    out_ref[...] = legendre_in(spec_ref[0, 0], leg_ref[0, 0], wave).reshape(YX, 1, 128)


def turn_in_kernel(got_ref, out_ref):
    out_ref[...] = turn(got_ref[...].reshape(YX, 128))[:ZC].reshape(ZC, 1, 128)


def grid_kernel(got_ref, factor_ref, outer_ref, cos_ref, sin_ref, rows_ref, out_ref):
    one, two, out = grid_rows(
        got_ref[...].reshape(ZC, 128), factor_ref, outer_ref, cos_ref, sin_ref
    )
    rows_ref[0] = one
    rows_ref[1] = two
    out_ref[...] = out.reshape(ZC, 1, 128)


def turn_out_kernel(got_ref, out_ref):
    got = jnp.concatenate([got_ref[...].reshape(ZC, 128), jnp.zeros((YX - ZC, 128), F32)], 0)
    out_ref[...] = turn(got).reshape(YX, 1, 128)


def legendre_out_kernel(wave_ref, weight_ref, got_ref, leg_ref, rows_ref, out_ref, grid_ref):
    for a in range(NA):
        grid_ref[0, :, a * NB : (a + 1) * NB] = rows_ref[:, a, :].astype(BF16)
    wave = wave_ref[:, :1].astype(jnp.int32)
    weight = weight_ref[...].reshape(1, NLAT)
    real, imag = legendre_out(got_ref[...].reshape(YX, 128), weight, leg_ref[0, 0], wave)
    out_ref[0, 0, :, :NDEG] = real.astype(BF16)
    out_ref[0, 0, :, NDEG:] = imag.astype(BF16)


VMEM = pl.BlockSpec(memory_space=pltpu.VMEM)
SMEM = pl.BlockSpec(memory_space=pltpu.SMEM)


def call(kernel, name, in_specs, outs, flops=10**6):
    single = not isinstance(outs, list)
    return pl.pallas_call(
        kernel,
        name=name,
        in_specs=in_specs,
        out_specs=VMEM if single else [VMEM] * len(outs),
        out_shape=outs if single else tuple(outs),
        compiler_params=pltpu.CompilerParams(vmem_limit_bytes=24 * 1024 * 1024),
        cost_estimate=pl.CostEstimate(flops=flops, bytes_accessed=100000, transcendentals=0),
    )


def shape(*dims, dtype=F32):
    return jax.ShapeDtypeStruct(dims, dtype)


def shards(spectral_in, legendre, slot_wave, row_length, quad_weight):
    lat_index = (lax.axis_index("z") * 8 + lax.axis_index("y")) * 2 + lax.axis_index("c")
    place = jnp.concatenate([jnp.stack([lax.axis_index("x"), lat_index]).astype(jnp.int32), row_length])
    wave, factor, outer, cosine, sine = call(
        tables_kernel,
        "tables",
        [SMEM, VMEM],
        [
            shape(1, 128),
            shape(8, SLOTS),
            shape(2, 2 * NA_PAD, 2 * SLOTS, dtype=BF16),
            shape(2, 24, SLOTS),
            shape(2, 24, SLOTS),
        ],
        2 * 10**9,
    )(place, slot_wave)
    to_send = call(legendre_in_kernel, "legendre_in", [VMEM] * 3, shape(YX, 1, 128))(
        wave, spectral_in, legendre
    )
    got = lax.all_to_all(to_send, ("x", "y"), 0, 0, tiled=True)
    to_send = call(turn_in_kernel, "turn_in", [VMEM], shape(ZC, 1, 128))(got)
    got = lax.all_to_all(to_send, ("z", "c"), 0, 0, tiled=True)
    rows, to_send = call(
        grid_kernel, "grid", [VMEM] * 5, [shape(2, NA_PAD, NB), shape(ZC, 1, 128)]
    )(got, factor, outer, cosine, sine)
    got = lax.all_to_all(to_send, ("z", "c"), 0, 0, tiled=True)
    to_send = call(turn_out_kernel, "turn_out", [VMEM], shape(YX, 1, 128))(got)
    got = lax.all_to_all(to_send, ("x", "y"), 0, 0, tiled=True)
    spectral_out, grid_field = call(
        legendre_out_kernel,
        "legendre_out",
        [VMEM] * 5,
        [shape(1, 1, 4, 2 * NDEG, dtype=BF16), shape(1, 2, NLON, dtype=BF16)],
    )(wave, quad_weight, got, legendre, rows)
    return grid_field, spectral_out


def solution(mesh):
    cut = Mesh(mesh.devices.reshape(12, 8, 2, 4), ("z", "y", "c", "x"))
    lat = ("z", "y", "c")
    in_specs = (P("x", lat, None, None), P("x", lat, None, None), P(), P(lat), P())
    out_specs = (P("x", lat, None), P("x", lat, None, None))
    return jax.shard_map(shards, mesh=cut, in_specs=in_specs, out_specs=out_specs, check_vma=False)
```

time: 77.9 us -> 75.5 us (0.969)
  Pallas kernels: 5.21 us -> 3.84 us
  blocking collectives: 71 us -> 69.9 us
    all_to_all x2, blocking collectives: 41.4 us -> 39.4 us  [shards(): got = lax.all_to_all(to_send, ('z', 'c'), 0, 0, tiled=True)]
    pallas_call x6, Pallas kernels: 5.21 us -> 3.84 us  [the longest x1 1.17 us: shards(): call(tables_kernel, 'tables', [SMEM, VMEM], [shape(1, 128), shape(8, SLOT...]
    all_to_all x2, blocking collectives: 29.6 us -> 30.5 us  [shards(): got = lax.all_to_all(to_send, ('x', 'y'), 0, 0, tiled=True)]
where the time goes in v3:
time: 75.5 us; the launch traced here: 75.2 us
  blocking collectives  69.9 us (93%)
  Pallas kernels  3.84 us (5%)
    all_to_all x2, blocking collectives, shards(): got = lax.all_to_all(to_send, ('z', 'c'), 0, 0, tiled=True)  39.4 us
    all_to_all x2, blocking collectives, shards(): got = lax.all_to_all(to_send, ('x', 'y'), 0, 0, tiled=True)  30.5 us

profile of v3, /device:TPU:1, one launch (start us, length us, event | category | flops | bytes accessed | tf_op | source)
XLA Modules:
  0.0 75.2 jit_solution(10461424673291123890)
XLA Ops:
  0.6 0.0 copy-start.3
  0.7 0.0 copy-start.4
  0.7 0.7 copy-done.4
  1.3 0.1 pad_add_fusion.place_ref
  1.4 0.0 copy-done.3
  1.4 0.0 copy-start
  1.4 0.0 copy-start.1
  1.4 1.2 %tables.1 = (f32[1,128]{1,0:T(1,128)S(1)}, f32[8,768]{1,0:T(8,128)S(1)}, bf16[2,48,1536]{2,1,0:T(8,128)(2,1)S(1)}, f32[2,24,768]{2,1,0:T(8,128)S(1)}, f32[2,24,768]{2,1,0:T(8,128)S(1)}) custom-call(s32[4]{0:T(128)S(1)} %pad_add_fusion.place_ref, s32[4,192]{1,0:T(4,128)S(1)} %copy-done.3), custom_call_target="tpu_custom_call" | custom-call | flops 2000000000 | bytes 100000 | tf_op jit(solution)/shard_map/tables/pallas_call | solution.py:275
  2.6 0.0 copy-done
  2.6 0.0 copy-done.1
  2.6 0.4 legendre_in.1
  3.0 18.9 %all_to_all.20.got_ref = f32[32,1,128]{2,1,0:T(1,128)S(1)} all-to-all(f32[32,1,128]{2,1,0:T(1,128)S(1)} %legendre_in.1), channel_id=1, replica_groups=mesh['z'=12,'y'=8,'c'=2,'x'=4] {'x','y'}, dimensions={0} | all-to-all | bytes 32768 | tf_op jit(solution)/shard_map/all_to_all | solution.py:291
  21.9 0.1 turn_in.1
  22.0 26.5 %all_to_all.21.got_ref = f32[24,1,128]{2,1,0:T(1,128)S(1)} all-to-all(f32[24,1,128]{2,1,0:T(1,128)S(1)} %turn_in.1), channel_id=1, replica_groups=mesh['z'=12,'y'=8,'c'=2,'x'=4] {'z','c'}, dimensions={0} | all-to-all | bytes 24576 | tf_op jit(solution)/shard_map/all_to_all | solution.py:293
  48.5 1.0 %grid.1 = (f32[2,24,128]{2,1,0:T(8,128)S(1)}, f32[24,1,128]{2,1,0:T(1,128)S(1)}) custom-call(f32[24,1,128]{2,1,0:T(1,128)S(1)} %all_to_all.21.got_ref, f32[8,768]{1,0:T(8,128)S(1)} %get-tuple-element.12.factor_ref, bf16[2,48,1536]{2,1,0:T(8,128)(2,1)S(1)} %get-tuple-element.13.outer_ref, f32[2,24,768]{2,1,0:T(8,128)S(1)} %get-tuple-element.14.cos_ref, ...), custom_call_target="tpu_custom_call" | custom-call | flops 1000000 | bytes 100000 | tf_op jit(solution)/shard_map/grid/pallas_call | solution.py:294
  49.6 0.0 copy-start.2
  49.6 12.9 %all_to_all.22.got_ref = f32[24,1,128]{2,1,0:T(1,128)S(1)} all-to-all(f32[24,1,128]{2,1,0:T(1,128)S(1)} %get-tuple-element.16), channel_id=1, replica_groups=mesh['z'=12,'y'=8,'c'=2,'x'=4] {'z','c'}, dimensions={0} | all-to-all | bytes 24576 | tf_op jit(solution)/shard_map/all_to_all | solution.py:297
  62.5 0.1 turn_out.1
  62.6 11.6 %all_to_all.23.got_ref = f32[32,1,128]{2,1,0:T(1,128)S(1)} all-to-all(f32[32,1,128]{2,1,0:T(1,128)S(1)} %turn_out.1), channel_id=1, replica_groups=mesh['z'=12,'y'=8,'c'=2,'x'=4] {'x','y'}, dimensions={0} | all-to-all | bytes 32768 | tf_op jit(solution)/shard_map/all_to_all | solution.py:299
  74.2 0.0 copy-done.2
  74.2 1.0 %legendre_out.1 = (bf16[1,1,4,1280]{3,2,1,0:T(4,128)(2,1)}, bf16[1,2,2688]{2,1,0:T(2,128)(2,1)}) custom-call(f32[1,128]{1,0:T(1,128)S(1)} %get-tuple-element.11.wave_ref, f32[384]{0:T(512)S(1)} %copy-done.2, f32[32,1,128]{2,1,0:T(1,128)S(1)} %all_to_all.23.got_ref, bf16[1,1,640,384]{3,2,1,0:T(8,128)(2,1)S(1)} %copy-done, ...), custom_call_target="tpu_custom_call" | custom-call | flops 1000000 | bytes 100000 | tf_op jit(solution)/shard_map/legendre_out/pallas_call | solution.py:300
Async XLA Ops:
  0.6 0.8 copy-start.3
  0.7 0.7 copy-start.4
  1.4 1.2 %copy-start = (bf16[1,1,640,384]{3,2,1,0:T(8,128)(2,1)S(1)}, bf16[1,1,640,384]{3,2,1,0:T(8,128)(2,1)}, u32[]{:S(2)}) copy-start(bf16[1,1,640,384]{3,2,1,0:T(8,128)(2,1)} %leg_ref.3) | copy-start | bytes 1474564
  1.4 1.2 %copy-start.1 = (bf16[1,1,4,1280]{3,2,1,0:T(4,128)(2,1)S(1)}, bf16[1,1,4,1280]{3,2,1,0:T(4,128)(2,1)}, u32[]{:S(2)}) copy-start(bf16[1,1,4,1280]{3,2,1,0:T(4,128)(2,1)} %spec_ref.1) | copy-start | bytes 30724
  49.6 24.6 %copy-start.2 = (f32[384]{0:T(512)S(1)}, f32[384]{0:T(512)}, u32[]{:S(2)}) copy-start(f32[384]{0:T(512)} %weight_ref.1) | copy-start | bytes 4612

commit v4 on v3

--- a/solution.py
+++ b/solution.py
@@ -44,20 +44,20 @@
     return one_hot((lane & 63) == ((l & 1) * 32 + (l >> 5) * 2 + ((l >> 1) & 1)))
 
 
-def legendre_in(spec, leg, wave):
+def legendre_in(spec, leg, wave, select):
     both = jnp.concatenate([spec[:, :NDEG].astype(F32), spec[:, NDEG:].astype(F32)], 0)
     kept = jnp.where(iota(both.shape, 1) >= wave, both, 0.0).astype(BF16)
     four = dot(kept, leg).astype(BF16).astype(F32)
     mine = ((iota((8, NLAT), 1) >> 2) & 7) == iota((8, NLAT), 0)
     spread = jnp.concatenate([jnp.where(mine, four[q : q + 1], 0.0) for q in range(8)], 0)
-    moved = dot(spread.astype(BF16), row_selector())
+    moved = dot(spread.astype(BF16), select)
     return jnp.where(iota((YX, 128), 1) < 64, moved[:YX], moved[YX:])
 
 
-def legendre_out(got, weight, leg, wave):
+def legendre_out(got, weight, leg, wave, select):
     low = iota((YX, 128), 1) < 64
     spread = jnp.concatenate([jnp.where(low, got, 0.0), jnp.where(low, 0.0, got)], 0)
-    moved = dot(spread.astype(BF16), row_selector(), ((1,), (1,)))
+    moved = dot(spread.astype(BF16), select, ((1,), (1,)))
     mine = ((iota((8, NLAT), 1) >> 2) & 7) == iota((8, NLAT), 0)
     rows = [
         jnp.sum(jnp.where(mine, moved[q * 8 : (q + 1) * 8], 0.0), 0, keepdims=True) for q in range(8)
@@ -92,10 +92,13 @@
     return out
 
 
-def slot_order(waves):
+def slot_selector():
     k = iota((192, 128), 0) & 31
     lane = iota((192, 128), 1)
-    pick = one_hot(k == ((lane >> 6) * 16 + (lane & 7) * 2 + ((lane >> 5) & 1)))
+    return one_hot(k == ((lane >> 6) * 16 + (lane & 7) * 2 + ((lane >> 5) & 1)))
+
+
+def slot_order(waves, pick):
     both = jnp.concatenate([(waves >> 3).astype(F32), (waves & 7).astype(F32)], 0)
     part = iota((8, 192), 1) >> 5
     spread = jnp.concatenate([jnp.where(part == q, both, 0.0) for q in range(6)], 0)
@@ -148,7 +151,7 @@
     empty = waves >= float(M)
     rows = [jnp.where(empty, 0.0, jnp.where(waves == 0.0, 1.0, 2.0))]
     rows += [jnp.where(empty, 0.0, 1.0 / n) for n in lengths]
-    rows += [jnp.full_like(waves, n) for n in lengths]
+    rows += [jnp.broadcast_to(n, waves.shape) for n in lengths]
     return jnp.concatenate(rows + [jnp.zeros((3, SLOTS), F32)], 0)
 
 
@@ -202,22 +205,29 @@
     return grids[0], grids[1], back.astype(BF16).astype(F32)
 
 
-def tables_kernel(place_ref, waves_ref, wave_ref, factor_ref, outer_ref, cos_ref, sin_ref):
+def select_kernel(pick_ref, select_ref):
+    pick_ref[...] = slot_selector()
+    select_ref[...] = row_selector()
+
+
+def tables_kernel(place_ref, waves_ref, length_ref, pick_ref, wave_ref, factor_ref, outer_ref, cos_ref, sin_ref):
     waves = waves_ref[...]
-    here = (iota((4, 192), 0) == place_ref[0]) & (iota((4, 192), 1) == place_ref[1])
+    place = place_ref[...].reshape(1, 2)
+    length = length_ref[...].reshape(1, 2)
+    here = (iota((4, 192), 0) == place[:, :1]) & (iota((4, 192), 1) == place[:, 1:2])
     own = jnp.where(here, waves.astype(F32), 0.0)
     own = jnp.sum(jnp.sum(own, 0, keepdims=True), 1, keepdims=True)
     wave_ref[...] = jnp.broadcast_to(own, (1, 128))
-    order = slot_order(waves)
-    lengths = [place_ref[2 + r].astype(F32) for r in range(2)]
+    order = slot_order(waves, pick_ref[...])
+    lengths = [length[:, r : r + 1].astype(F32) for r in range(2)]
     factor_ref[...] = factors(order, lengths)
     for r in range(2):
         outer_ref[r], cos_ref[r], sin_ref[r] = tables(order, lengths[r])
 
 
-def legendre_in_kernel(wave_ref, spec_ref, leg_ref, out_ref):
+def legendre_in_kernel(wave_ref, select_ref, spec_ref, leg_ref, out_ref):
     wave = wave_ref[:, :1].astype(jnp.int32)
-    out_ref[...] = legendre_in(spec_ref[0, 0], leg_ref[0, 0], wave).reshape(YX, 1, 128)
+    out_ref[...] = legendre_in(spec_ref[0, 0], leg_ref[0, 0], wave, select_ref[...]).reshape(YX, 1, 128)
 
 
 def turn_in_kernel(got_ref, out_ref):
@@ -238,12 +248,12 @@
     out_ref[...] = turn(got).reshape(YX, 1, 128)
 
 
-def legendre_out_kernel(wave_ref, weight_ref, got_ref, leg_ref, rows_ref, out_ref, grid_ref):
+def legendre_out_kernel(wave_ref, select_ref, weight_ref, got_ref, leg_ref, rows_ref, out_ref, grid_ref):
     for a in range(NA):
         grid_ref[0, :, a * NB : (a + 1) * NB] = rows_ref[:, a, :].astype(BF16)
     wave = wave_ref[:, :1].astype(jnp.int32)
     weight = weight_ref[...].reshape(1, NLAT)
-    real, imag = legendre_out(got_ref[...].reshape(YX, 128), weight, leg_ref[0, 0], wave)
+    real, imag = legendre_out(got_ref[...].reshape(YX, 128), weight, leg_ref[0, 0], wave, select_ref[...])
     out_ref[0, 0, :, :NDEG] = real.astype(BF16)
     out_ref[0, 0, :, NDEG:] = imag.astype(BF16)
 
@@ -271,11 +281,14 @@
 
 def shards(spectral_in, legendre, slot_wave, row_length, quad_weight):
     lat_index = (lax.axis_index("z") * 8 + lax.axis_index("y")) * 2 + lax.axis_index("c")
-    place = jnp.concatenate([jnp.stack([lax.axis_index("x"), lat_index]).astype(jnp.int32), row_length])
+    place = jnp.stack([lax.axis_index("x"), lat_index]).astype(jnp.int32)
+    pick, select = call(
+        select_kernel, "select", [], [shape(192, 128, dtype=BF16), shape(NLAT, 128, dtype=BF16)], 2 * 10**9
+    )()
     wave, factor, outer, cosine, sine = call(
         tables_kernel,
         "tables",
-        [SMEM, VMEM],
+        [VMEM] * 4,
         [
             shape(1, 128),
             shape(8, SLOTS),
@@ -283,10 +296,10 @@
             shape(2, 24, SLOTS),
             shape(2, 24, SLOTS),
         ],
-        2 * 10**9,
-    )(place, slot_wave)
-    to_send = call(legendre_in_kernel, "legendre_in", [VMEM] * 3, shape(YX, 1, 128))(
-        wave, spectral_in, legendre
+        10**6,
+    )(place, slot_wave, row_length, pick)
+    to_send = call(legendre_in_kernel, "legendre_in", [VMEM] * 4, shape(YX, 1, 128))(
+        wave, select, spectral_in, legendre
     )
     got = lax.all_to_all(to_send, ("x", "y"), 0, 0, tiled=True)
     to_send = call(turn_in_kernel, "turn_in", [VMEM], shape(ZC, 1, 128))(got)
@@ -300,9 +313,9 @@
     spectral_out, grid_field = call(
         legendre_out_kernel,
         "legendre_out",
-        [VMEM] * 5,
+        [VMEM] * 6,
         [shape(1, 1, 4, 2 * NDEG, dtype=BF16), shape(1, 2, NLON, dtype=BF16)],
-    )(wave, quad_weight, got, legendre, rows)
+    )(wave, select, quad_weight, got, legendre, rows)
     return grid_field, spectral_out
 
 

time: 75.5 us -> 75 us (level)
    pallas_call x3 -> x4, Pallas kernels: 2.57 us -> 2.08 us  [the longest x1 1 us: shards(): call(legendre_out_kernel, 'legendre_out', [VMEM] * 6, [shape(1, 1, 4, 2 *...]
where the time goes in v4:
time: 75 us; the launch traced here: 74.7 us
  blocking collectives  69.9 us (93%)
  Pallas kernels  3.33 us (4%)
    all_to_all x2, blocking collectives, shards(): got = lax.all_to_all(to_send, ('z', 'c'), 0, 0, tiled=True)  39.4 us
    all_to_all x2, blocking collectives, shards(): got = lax.all_to_all(to_send, ('x', 'y'), 0, 0, tiled=True)  30.5 us

profile of v4, /device:TPU:1, one launch (start us, length us, event | category | flops | bytes accessed | tf_op | source)
XLA Modules:
  0.0 74.7 jit_solution(8260253779925470709)
XLA Ops:
  0.6 0.0 copy-start
  0.6 0.1 select.1
  0.7 0.0 copy-start.1
  0.8 0.0 copy-start.2
  0.8 0.1 pad_add_fusion.place_ref
  0.9 0.0 copy-start.4
  0.9 0.6 copy-done.2
  1.5 0.0 copy-done.4
  1.5 0.6 tables.1
  2.1 0.0 copy-done
  2.1 0.0 copy-done.1
  2.1 0.4 legendre_in.1
  2.5 18.9 %all_to_all.20.got_ref = f32[32,1,128]{2,1,0:T(1,128)S(1)} all-to-all(f32[32,1,128]{2,1,0:T(1,128)S(1)} %legendre_in.1), channel_id=1, replica_groups=mesh['z'=12,'y'=8,'c'=2,'x'=4] {'x','y'}, dimensions={0} | all-to-all | bytes 32768 | tf_op jit(solution)/shard_map/all_to_all | solution.py:304
  21.5 0.1 turn_in.1
  21.6 26.5 %all_to_all.21.got_ref = f32[24,1,128]{2,1,0:T(1,128)S(1)} all-to-all(f32[24,1,128]{2,1,0:T(1,128)S(1)} %turn_in.1), channel_id=1, replica_groups=mesh['z'=12,'y'=8,'c'=2,'x'=4] {'z','c'}, dimensions={0} | all-to-all | bytes 24576 | tf_op jit(solution)/shard_map/all_to_all | solution.py:306
  48.1 0.0 copy-start.3
  48.1 1.0 %grid.1 = (f32[2,24,128]{2,1,0:T(8,128)S(1)}, f32[24,1,128]{2,1,0:T(1,128)S(1)}) custom-call(f32[24,1,128]{2,1,0:T(1,128)S(1)} %all_to_all.21.got_ref, f32[8,768]{1,0:T(8,128)S(1)} %get-tuple-element.16.factor_ref, bf16[2,48,1536]{2,1,0:T(8,128)(2,1)S(1)} %get-tuple-element.17.outer_ref, f32[2,24,768]{2,1,0:T(8,128)S(1)} %get-tuple-element.18.cos_ref, ...), custom_call_target="tpu_custom_call" | custom-call | flops 1000000 | bytes 100000 | tf_op jit(solution)/shard_map/grid/pallas_call | solution.py:307
  49.1 12.9 %all_to_all.22.got_ref = f32[24,1,128]{2,1,0:T(1,128)S(1)} all-to-all(f32[24,1,128]{2,1,0:T(1,128)S(1)} %get-tuple-element.20), channel_id=1, replica_groups=mesh['z'=12,'y'=8,'c'=2,'x'=4] {'z','c'}, dimensions={0} | all-to-all | bytes 24576 | tf_op jit(solution)/shard_map/all_to_all | solution.py:310
  62.0 0.1 turn_out.1
  62.1 11.6 %all_to_all.23.got_ref = f32[32,1,128]{2,1,0:T(1,128)S(1)} all-to-all(f32[32,1,128]{2,1,0:T(1,128)S(1)} %turn_out.1), channel_id=1, replica_groups=mesh['z'=12,'y'=8,'c'=2,'x'=4] {'x','y'}, dimensions={0} | all-to-all | bytes 32768 | tf_op jit(solution)/shard_map/all_to_all | solution.py:312
  73.7 0.0 copy-done.3
  73.7 1.0 %legendre_out.1 = (bf16[1,1,4,1280]{3,2,1,0:T(4,128)(2,1)}, bf16[1,2,2688]{2,1,0:T(2,128)(2,1)}) custom-call(f32[1,128]{1,0:T(1,128)S(1)} %get-tuple-element.14.wave_ref, bf16[384,128]{1,0:T(8,128)(2,1)S(1)} %get-tuple-element.15.select_ref, f32[384]{0:T(512)S(1)} %copy-done.3, f32[32,1,128]{2,1,0:T(1,128)S(1)} %all_to_all.23.got_ref, ...), custom_call_target="tpu_custom_call" | custom-call | flops 1000000 | bytes 100000 | tf_op jit(solution)/shard_map/legendre_out/pallas_call | solution.py:313
Async XLA Ops:
  0.6 1.5 %copy-start = (bf16[1,1,640,384]{3,2,1,0:T(8,128)(2,1)S(1)}, bf16[1,1,640,384]{3,2,1,0:T(8,128)(2,1)}, u32[]{:S(2)}) copy-start(bf16[1,1,640,384]{3,2,1,0:T(8,128)(2,1)} %leg_ref.3) | copy-start | bytes 1474564
  0.7 1.4 %copy-start.1 = (bf16[1,1,4,1280]{3,2,1,0:T(4,128)(2,1)S(1)}, bf16[1,1,4,1280]{3,2,1,0:T(4,128)(2,1)}, u32[]{:S(2)}) copy-start(bf16[1,1,4,1280]{3,2,1,0:T(4,128)(2,1)} %spec_ref.1) | copy-start | bytes 30724
  0.8 0.7 copy-start.2
  0.9 0.7 copy-start.4
  48.1 25.6 %copy-start.3 = (f32[384]{0:T(512)S(1)}, f32[384]{0:T(512)}, u32[]{:S(2)}) copy-start(f32[384]{0:T(512)} %weight_ref.1) | copy-start | bytes 4612

commit v5 on v4

--- a/solution.py
+++ b/solution.py
@@ -210,24 +210,25 @@
     select_ref[...] = row_selector()
 
 
-def tables_kernel(place_ref, waves_ref, length_ref, pick_ref, wave_ref, factor_ref, outer_ref, cos_ref, sin_ref):
+def start_kernel(
+    waves_ref, length_ref, weight_ref, pick_ref, select_ref, spec_ref, leg_ref,
+    out_ref, wave_ref, line_ref, factor_ref, outer_ref, cos_ref, sin_ref,
+):
     waves = waves_ref[...]
-    place = place_ref[...].reshape(1, 2)
     length = length_ref[...].reshape(1, 2)
-    here = (iota((4, 192), 0) == place[:, :1]) & (iota((4, 192), 1) == place[:, 1:2])
+    lat_index = (lax.axis_index("z") * 8 + lax.axis_index("y")) * 2 + lax.axis_index("c")
+    here = (iota((4, 192), 0) == lax.axis_index("x")) & (iota((4, 192), 1) == lat_index)
     own = jnp.where(here, waves.astype(F32), 0.0)
     own = jnp.sum(jnp.sum(own, 0, keepdims=True), 1, keepdims=True)
     wave_ref[...] = jnp.broadcast_to(own, (1, 128))
+    line_ref[...] = weight_ref[...].reshape(1, NLAT)
     order = slot_order(waves, pick_ref[...])
     lengths = [length[:, r : r + 1].astype(F32) for r in range(2)]
     factor_ref[...] = factors(order, lengths)
     for r in range(2):
         outer_ref[r], cos_ref[r], sin_ref[r] = tables(order, lengths[r])
-
-
-def legendre_in_kernel(wave_ref, select_ref, spec_ref, leg_ref, out_ref):
-    wave = wave_ref[:, :1].astype(jnp.int32)
-    out_ref[...] = legendre_in(spec_ref[0, 0], leg_ref[0, 0], wave, select_ref[...]).reshape(YX, 1, 128)
+    out = legendre_in(spec_ref[0, 0], leg_ref[0, 0], own.astype(jnp.int32), select_ref[...])
+    out_ref[...] = out.reshape(YX, 1, 128)
 
 
 def turn_in_kernel(got_ref, out_ref):
@@ -252,8 +253,7 @@
     for a in range(NA):
         grid_ref[0, :, a * NB : (a + 1) * NB] = rows_ref[:, a, :].astype(BF16)
     wave = wave_ref[:, :1].astype(jnp.int32)
-    weight = weight_ref[...].reshape(1, NLAT)
-    real, imag = legendre_out(got_ref[...].reshape(YX, 128), weight, leg_ref[0, 0], wave, select_ref[...])
+    real, imag = legendre_out(got_ref[...].reshape(YX, 128), weight_ref[...], leg_ref[0, 0], wave, select_ref[...])
     out_ref[0, 0, :, :NDEG] = real.astype(BF16)
     out_ref[0, 0, :, NDEG:] = imag.astype(BF16)
 
@@ -280,27 +280,23 @@
 
 
 def shards(spectral_in, legendre, slot_wave, row_length, quad_weight):
-    lat_index = (lax.axis_index("z") * 8 + lax.axis_index("y")) * 2 + lax.axis_index("c")
-    place = jnp.stack([lax.axis_index("x"), lat_index]).astype(jnp.int32)
     pick, select = call(
         select_kernel, "select", [], [shape(192, 128, dtype=BF16), shape(NLAT, 128, dtype=BF16)], 2 * 10**9
     )()
-    wave, factor, outer, cosine, sine = call(
-        tables_kernel,
-        "tables",
-        [VMEM] * 4,
+    to_send, wave, weight, factor, outer, cosine, sine = call(
+        start_kernel,
+        "start",
+        [VMEM] * 7,
         [
+            shape(YX, 1, 128),
             shape(1, 128),
+            shape(1, NLAT),
             shape(8, SLOTS),
             shape(2, 2 * NA_PAD, 2 * SLOTS, dtype=BF16),
             shape(2, 24, SLOTS),
             shape(2, 24, SLOTS),
         ],
-        10**6,
-    )(place, slot_wave, row_length, pick)
-    to_send = call(legendre_in_kernel, "legendre_in", [VMEM] * 4, shape(YX, 1, 128))(
-        wave, select, spectral_in, legendre
-    )
+    )(slot_wave, row_length, quad_weight, pick, select, spectral_in, legendre)
     got = lax.all_to_all(to_send, ("x", "y"), 0, 0, tiled=True)
     to_send = call(turn_in_kernel, "turn_in", [VMEM], shape(ZC, 1, 128))(got)
     got = lax.all_to_all(to_send, ("z", "c"), 0, 0, tiled=True)
@@ -315,7 +311,7 @@
         "legendre_out",
         [VMEM] * 6,
         [shape(1, 1, 4, 2 * NDEG, dtype=BF16), shape(1, 2, NLON, dtype=BF16)],
-    )(wave, select, quad_weight, got, legendre, rows)
+    )(wave, select, weight, got, legendre, rows)
     return grid_field, spectral_out
 
 

time: 75 us -> 74.9 us (level)
  no operation moved by 1% of the time
where the time goes in v5:
time: 74.9 us; the launch traced here: 74.6 us
  blocking collectives  69.9 us (93%)
  Pallas kernels  3.08 us (4%)
  local copies, waits for them, and re-layouts  0.9 us (1%)
    all_to_all x2, blocking collectives, shards(): got = lax.all_to_all(to_send, ('z', 'c'), 0, 0, tiled=True)  39.4 us
    all_to_all x2, blocking collectives, shards(): got = lax.all_to_all(to_send, ('x', 'y'), 0, 0, tiled=True)  30.5 us

profile of v5, /device:TPU:1, one launch (start us, length us, event | category | flops | bytes accessed | tf_op | source)
XLA Modules:
  0.0 74.6 jit_solution(14807555748348928874)
XLA Ops:
  0.6 0.0 copy-start
  0.6 0.0 copy-start.1
  0.6 0.0 copy-start.2
  0.7 0.1 select.1
  0.8 0.0 copy-start.3
  0.8 0.0 copy-start.4
  0.8 0.9 %copy-done = bf16[1,1,640,384]{3,2,1,0:T(8,128)(2,1)S(1)} copy-done((bf16[1,1,640,384]{3,2,1,0:T(8,128)(2,1)S(1)}, bf16[1,1,640,384]{3,2,1,0:T(8,128)(2,1)}, u32[]{:S(2)}) %copy-start) | copy-done | bytes 491544
  1.7 0.0 copy-done.1
  1.7 0.0 copy-done.2
  1.7 0.0 copy-done.3
  1.7 0.0 copy-done.4
  1.7 0.7 start.1
  2.4 18.9 %all_to_all.20.got_ref = f32[32,1,128]{2,1,0:T(1,128)S(1)} all-to-all(f32[32,1,128]{2,1,0:T(1,128)S(1)} %get-tuple-element.19), channel_id=1, replica_groups=mesh['z'=12,'y'=8,'c'=2,'x'=4] {'x','y'}, dimensions={0} | all-to-all | bytes 32768 | tf_op jit(solution)/shard_map/all_to_all | solution.py:300
  21.4 0.1 turn_in.1
  21.5 26.5 %all_to_all.21.got_ref = f32[24,1,128]{2,1,0:T(1,128)S(1)} all-to-all(f32[24,1,128]{2,1,0:T(1,128)S(1)} %turn_in.1), channel_id=1, replica_groups=mesh['z'=12,'y'=8,'c'=2,'x'=4] {'z','c'}, dimensions={0} | all-to-all | bytes 24576 | tf_op jit(solution)/shard_map/all_to_all | solution.py:302
  48.0 1.0 %grid.1 = (f32[2,24,128]{2,1,0:T(8,128)S(1)}, f32[24,1,128]{2,1,0:T(1,128)S(1)}) custom-call(f32[24,1,128]{2,1,0:T(1,128)S(1)} %all_to_all.21.got_ref, f32[8,768]{1,0:T(8,128)S(1)} %get-tuple-element.20.factor_ref, bf16[2,48,1536]{2,1,0:T(8,128)(2,1)S(1)} %get-tuple-element.21.outer_ref, f32[2,24,768]{2,1,0:T(8,128)S(1)} %get-tuple-element.22.cos_ref, ...), custom_call_target="tpu_custom_call" | custom-call | flops 1000000 | bytes 100000 | tf_op jit(solution)/shard_map/grid/pallas_call | solution.py:303
  49.0 12.9 %all_to_all.22.got_ref = f32[24,1,128]{2,1,0:T(1,128)S(1)} all-to-all(f32[24,1,128]{2,1,0:T(1,128)S(1)} %get-tuple-element.24), channel_id=1, replica_groups=mesh['z'=12,'y'=8,'c'=2,'x'=4] {'z','c'}, dimensions={0} | all-to-all | bytes 24576 | tf_op jit(solution)/shard_map/all_to_all | solution.py:306
  61.9 0.1 turn_out.1
  62.0 11.6 %all_to_all.23.got_ref = f32[32,1,128]{2,1,0:T(1,128)S(1)} all-to-all(f32[32,1,128]{2,1,0:T(1,128)S(1)} %turn_out.1), channel_id=1, replica_groups=mesh['z'=12,'y'=8,'c'=2,'x'=4] {'x','y'}, dimensions={0} | all-to-all | bytes 32768 | tf_op jit(solution)/shard_map/all_to_all | solution.py:308
  73.6 1.0 %legendre_out.1 = (bf16[1,1,4,1280]{3,2,1,0:T(4,128)(2,1)}, bf16[1,2,2688]{2,1,0:T(2,128)(2,1)}) custom-call(f32[1,128]{1,0:T(1,128)S(1)} %get-tuple-element.17.wave_ref, bf16[384,128]{1,0:T(8,128)(2,1)S(1)} %get-tuple-element.16.select_ref, f32[1,384]{1,0:T(1,128)S(1)} %get-tuple-element.18.weight_ref, f32[32,1,128]{2,1,0:T(1,128)S(1)} %all_to_all.23.got_ref, ...), custom_call_target="tpu_custom_call" | custom-call | flops 1000000 | bytes 100000 | tf_op jit(solution)/shard_map/legendre_out/pallas_call | solution.py:309
Async XLA Ops:
  0.6 1.0 %copy-start = (bf16[1,1,640,384]{3,2,1,0:T(8,128)(2,1)S(1)}, bf16[1,1,640,384]{3,2,1,0:T(8,128)(2,1)}, u32[]{:S(2)}) copy-start(bf16[1,1,640,384]{3,2,1,0:T(8,128)(2,1)} %leg_ref.3) | copy-start | bytes 1474564
  0.6 1.0 %copy-start.1 = (bf16[1,1,4,1280]{3,2,1,0:T(4,128)(2,1)S(1)}, bf16[1,1,4,1280]{3,2,1,0:T(4,128)(2,1)}, u32[]{:S(2)}) copy-start(bf16[1,1,4,1280]{3,2,1,0:T(4,128)(2,1)} %spec_ref.1) | copy-start | bytes 30724
  0.6 1.0 %copy-start.2 = (s32[4,192]{1,0:T(4,128)S(1)}, s32[4,192]{1,0:T(4,128)}, u32[]{:S(2)}) copy-start(s32[4,192]{1,0:T(4,128)} %waves_ref.1) | copy-start | bytes 9220
  0.8 0.9 %copy-start.3 = (f32[384]{0:T(512)S(1)}, f32[384]{0:T(512)}, u32[]{:S(2)}) copy-start(f32[384]{0:T(512)} %weight_ref.1) | copy-start | bytes 4612
  0.8 0.9 %copy-start.4 = (s32[2]{0:T(128)S(1)}, s32[2]{0:T(128)}, u32[]{:S(2)}) copy-start(s32[2]{0:T(128)} %length_ref.1) | copy-start | bytes 28

commit v6 on v5

--- a/solution.py
+++ b/solution.py
@@ -210,25 +210,24 @@
     select_ref[...] = row_selector()
 
 
-def start_kernel(
-    waves_ref, length_ref, weight_ref, pick_ref, select_ref, spec_ref, leg_ref,
-    out_ref, wave_ref, line_ref, factor_ref, outer_ref, cos_ref, sin_ref,
-):
-    waves = waves_ref[...]
-    length = length_ref[...].reshape(1, 2)
+def legendre_in_kernel(waves_ref, weight_ref, select_ref, spec_ref, leg_ref, out_ref, wave_ref, line_ref):
     lat_index = (lax.axis_index("z") * 8 + lax.axis_index("y")) * 2 + lax.axis_index("c")
     here = (iota((4, 192), 0) == lax.axis_index("x")) & (iota((4, 192), 1) == lat_index)
-    own = jnp.where(here, waves.astype(F32), 0.0)
+    own = jnp.where(here, waves_ref[...].astype(F32), 0.0)
     own = jnp.sum(jnp.sum(own, 0, keepdims=True), 1, keepdims=True)
     wave_ref[...] = jnp.broadcast_to(own, (1, 128))
     line_ref[...] = weight_ref[...].reshape(1, NLAT)
-    order = slot_order(waves, pick_ref[...])
+    out = legendre_in(spec_ref[0, 0], leg_ref[0, 0], own.astype(jnp.int32), select_ref[...])
+    out_ref[...] = out.reshape(YX, 1, 128)
+
+
+def tables_kernel(waves_ref, length_ref, pick_ref, factor_ref, outer_ref, cos_ref, sin_ref):
+    length = length_ref[...].reshape(1, 2)
+    order = slot_order(waves_ref[...], pick_ref[...])
     lengths = [length[:, r : r + 1].astype(F32) for r in range(2)]
     factor_ref[...] = factors(order, lengths)
     for r in range(2):
         outer_ref[r], cos_ref[r], sin_ref[r] = tables(order, lengths[r])
-    out = legendre_in(spec_ref[0, 0], leg_ref[0, 0], own.astype(jnp.int32), select_ref[...])
-    out_ref[...] = out.reshape(YX, 1, 128)
 
 
 def turn_in_kernel(got_ref, out_ref):
@@ -283,20 +282,21 @@
     pick, select = call(
         select_kernel, "select", [], [shape(192, 128, dtype=BF16), shape(NLAT, 128, dtype=BF16)], 2 * 10**9
     )()
-    to_send, wave, weight, factor, outer, cosine, sine = call(
-        start_kernel,
-        "start",
-        [VMEM] * 7,
+    to_send, wave, weight = call(
+        legendre_in_kernel, "legendre_in", [VMEM] * 5, [shape(YX, 1, 128), shape(1, 128), shape(1, NLAT)]
+    )(slot_wave, quad_weight, select, spectral_in, legendre)
+    factor, outer, cosine, sine = call(
+        tables_kernel,
+        "tables",
+        [VMEM] * 3,
         [
-            shape(YX, 1, 128),
-            shape(1, 128),
-            shape(1, NLAT),
             shape(8, SLOTS),
             shape(2, 2 * NA_PAD, 2 * SLOTS, dtype=BF16),
             shape(2, 24, SLOTS),
             shape(2, 24, SLOTS),
         ],
-    )(slot_wave, row_length, quad_weight, pick, select, spectral_in, legendre)
+        2 * 10**9,
+    )(slot_wave, row_length, pick)
     got = lax.all_to_all(to_send, ("x", "y"), 0, 0, tiled=True)
     to_send = call(turn_in_kernel, "turn_in", [VMEM], shape(ZC, 1, 128))(got)
     got = lax.all_to_all(to_send, ("z", "c"), 0, 0, tiled=True)

time: 74.9 us -> 75.4 us (level)
  blocking collectives: 69.9 us -> 43.4 us
  starting transfers between devices: 0 us -> 17.3 us
  waiting for transfers between devices: 0 us -> 8.15 us
  Pallas kernels: 3.08 us -> 3.94 us
    all_to_all x2 -> x1, blocking collectives: 39.4 us -> 12.9 us  [shards(): got = lax.all_to_all(to_send, ('z', 'c'), 0, 0, tiled=True)]
    all_to_all x0 -> x1, starting transfers between devices: none -> 17.3 us  [shards(): got = lax.all_to_all(to_send, ('z', 'c'), 0, 0, tiled=True)]
    all_to_all x0 -> x1, waiting for transfers between devices: none -> 8.15 us  [shards(): got = lax.all_to_all(to_send, ('z', 'c'), 0, 0, tiled=True)]
  transfers between devices with their start and end apart: 0 -> 1, of which waited for: 0 -> 1; matrix products, arithmetic and copies ran while one was open for 0% -> 0% of each run, Pallas kernels for 0% -> 1%
where the time goes in v6:
time: 75.4 us; the launch traced here: 75.1 us
  blocking collectives  43.4 us (58%)
  starting transfers between devices  17.3 us (23%)
  waiting for transfers between devices  8.15 us (11%)
  Pallas kernels  3.94 us (5%)
  local copies, waits for them, and re-layouts  1.57 us (2%)
    all_to_all x2, blocking collectives, shards(): got = lax.all_to_all(to_send, ('x', 'y'), 0, 0, tiled=True)  30.5 us
    all_to_all x1, starting transfers between devices, shards(): got = lax.all_to_all(to_send, ('z', 'c'), 0, 0, tiled=True)  17.3 us
    all_to_all x1, blocking collectives, shards(): got = lax.all_to_all(to_send, ('z', 'c'), 0, 0, tiled=True)  12.9 us
    all_to_all x1, waiting for transfers between devices, shards(): got = lax.all_to_all(to_send, ('z', 'c'), 0, 0, tiled=True)  8.15 us
    unnamed x10, local copies, waits for them, and re-layouts  1.57 us
  transfers between devices with their start and end apart: 1, of which 1 were waited for; matrix products, arithmetic and copies ran while one was open for 0% of the time, Pallas kernels for 1%

profile of v6, /device:TPU:1, one launch (start us, length us, event | category | flops | bytes accessed | tf_op | source)
XLA Modules:
  0.0 75.1 jit_solution(16476401923271928893)
XLA Ops:
  0.6 0.0 copy-start.1
  0.6 0.0 copy-start
  0.7 0.0 copy-start.2
  0.7 0.0 copy-start.3
  0.7 0.1 select.1
  0.8 0.6 copy-done.1
  1.3 0.3 copy-done
  1.7 0.0 copy-done.2
  1.7 0.0 copy-done.3
  1.7 0.4 legendre_in.1
  2.1 18.9 %all_to_all.20.got_ref = f32[32,1,128]{2,1,0:T(1,128)S(1)} all-to-all(f32[32,1,128]{2,1,0:T(1,128)S(1)} %get-tuple-element.18), channel_id=1, replica_groups=mesh['z'=12,'y'=8,'c'=2,'x'=4] {'x','y'}, dimensions={0} | all-to-all | bytes 32768 | tf_op jit(solution)/shard_map/all_to_all | solution.py:300
  21.1 0.7 turn_in.1
  21.8 17.3 %all-to-all-start.1 = ((f32[24,1,128]{2,1,0:T(1,128)}), f32[24,1,128]{2,1,0:T(1,128)S(1)}, u32[]{:S(2)}, u32[]{:S(2)}) async-start(f32[24,1,128]{2,1,0:T(1,128)} %turn_in.1), calls=%async_computation.1 | async-start | bytes 24576 | tf_op jit(solution)/shard_map/all_to_all | solution.py:302
  39.1 0.0 copy-start.4
  39.1 0.6 copy-done.4
  39.7 0.6 tables.1
  40.3 8.2 %all-to-all-done.1.got_ref = f32[24,1,128]{2,1,0:T(1,128)S(1)} async-done(((f32[24,1,128]{2,1,0:T(1,128)}), f32[24,1,128]{2,1,0:T(1,128)S(1)}, u32[]{:S(2)}, u32[]{:S(2)}) %all-to-all-start.1) | async-done | bytes 12320 | tf_op jit(solution)/shard_map/all_to_all | solution.py:302
  48.5 1.0 %grid.1 = (f32[2,24,128]{2,1,0:T(8,128)S(1)}, f32[24,1,128]{2,1,0:T(1,128)S(1)}) custom-call(f32[24,1,128]{2,1,0:T(1,128)S(1)} %all-to-all-done.1.got_ref, f32[8,768]{1,0:T(8,128)S(1)} %get-tuple-element.20.factor_ref, bf16[2,48,1536]{2,1,0:T(8,128)(2,1)S(1)} %get-tuple-element.21.outer_ref, f32[2,24,768]{2,1,0:T(8,128)S(1)} %get-tuple-element.22.cos_ref, ...), custom_call_target="tpu_custom_call" | custom-call | flops 1000000 | bytes 100000 | tf_op jit(solution)/shard_map/grid/pallas_call | solution.py:303
  49.5 12.9 %all_to_all.21.got_ref = f32[24,1,128]{2,1,0:T(1,128)S(1)} all-to-all(f32[24,1,128]{2,1,0:T(1,128)S(1)} %get-tuple-element.24), channel_id=1, replica_groups=mesh['z'=12,'y'=8,'c'=2,'x'=4] {'z','c'}, dimensions={0} | all-to-all | bytes 24576 | tf_op jit(solution)/shard_map/all_to_all | solution.py:306
  62.4 0.1 turn_out.1
  62.5 11.6 %all_to_all.22.got_ref = f32[32,1,128]{2,1,0:T(1,128)S(1)} all-to-all(f32[32,1,128]{2,1,0:T(1,128)S(1)} %turn_out.1), channel_id=1, replica_groups=mesh['z'=12,'y'=8,'c'=2,'x'=4] {'x','y'}, dimensions={0} | all-to-all | bytes 32768 | tf_op jit(solution)/shard_map/all_to_all | solution.py:308
  74.1 1.0 %legendre_out.1 = (bf16[1,1,4,1280]{3,2,1,0:T(4,128)(2,1)}, bf16[1,2,2688]{2,1,0:T(2,128)(2,1)}) custom-call(f32[1,128]{1,0:T(1,128)S(1)} %get-tuple-element.16.wave_ref, bf16[384,128]{1,0:T(8,128)(2,1)S(1)} %get-tuple-element.15.select_ref, f32[1,384]{1,0:T(1,128)S(1)} %get-tuple-element.17.weight_ref, f32[32,1,128]{2,1,0:T(1,128)S(1)} %all_to_all.22.got_ref, ...), custom_call_target="tpu_custom_call" | custom-call | flops 1000000 | bytes 100000 | tf_op jit(solution)/shard_map/legendre_out/pallas_call | solution.py:309
Async XLA Ops:
  0.6 0.7 copy-start.1
  0.6 1.0 %copy-start = (bf16[1,1,640,384]{3,2,1,0:T(8,128)(2,1)S(1)}, bf16[1,1,640,384]{3,2,1,0:T(8,128)(2,1)}, u32[]{:S(2)}) copy-start(bf16[1,1,640,384]{3,2,1,0:T(8,128)(2,1)} %leg_ref.3) | copy-start | bytes 1474564
  0.7 1.0 %copy-start.2 = (s32[4,192]{1,0:T(4,128)S(1)}, s32[4,192]{1,0:T(4,128)}, u32[]{:S(2)}) copy-start(s32[4,192]{1,0:T(4,128)} %waves_ref.3) | copy-start | bytes 9220
  0.7 1.0 %copy-start.3 = (f32[384]{0:T(512)S(1)}, f32[384]{0:T(512)}, u32[]{:S(2)}) copy-start(f32[384]{0:T(512)} %weight_ref.1) | copy-start | bytes 4612
  21.8 26.7 %all-to-all-start.1 = ((f32[24,1,128]{2,1,0:T(1,128)}), f32[24,1,128]{2,1,0:T(1,128)S(1)}, u32[]{:S(2)}, u32[]{:S(2)}) async-start(f32[24,1,128]{2,1,0:T(1,128)} %turn_in.1), calls=%async_computation.1 | async-start | bytes 24576 | tf_op jit(solution)/shard_map/all_to_all | solution.py:302
  39.1 0.7 copy-start.4

commit v7 on v5

--- a/solution.py
+++ b/solution.py
@@ -41,7 +41,7 @@
 def row_selector():
     l = iota((NLAT, 128), 0)
     lane = iota((NLAT, 128), 1)
-    return one_hot((lane & 63) == ((l & 1) * 32 + (l >> 5) * 2 + ((l >> 1) & 1)))
+    return one_hot((lane & 63) == ((l & 1) * 32 + ((l >> 1) & 1) * 12 + (l >> 5)))
 
 
 def legendre_in(spec, leg, wave, select):
@@ -93,14 +93,15 @@
 
 
 def slot_selector():
-    k = iota((192, 128), 0) & 31
+    k = iota((192, 128), 0) & 62
     lane = iota((192, 128), 1)
-    return one_hot(k == ((lane >> 6) * 16 + (lane & 7) * 2 + ((lane >> 5) & 1)))
+    return one_hot(k == ((lane >> 5) * 16 + (lane & 7) * 2))
 
 
 def slot_order(waves, pick):
     both = jnp.concatenate([(waves >> 3).astype(F32), (waves & 7).astype(F32)], 0)
-    part = iota((8, 192), 1) >> 5
+    k = iota((8, 192), 1)
+    part = (k >> 6) + (k & 1) * 3
     spread = jnp.concatenate([jnp.where(part == q, both, 0.0) for q in range(6)], 0)
     moved = dot(spread.astype(BF16), pick)
     row = iota((8, 128), 0)
@@ -299,11 +300,11 @@
     )(slot_wave, row_length, quad_weight, pick, select, spectral_in, legendre)
     got = lax.all_to_all(to_send, ("x", "y"), 0, 0, tiled=True)
     to_send = call(turn_in_kernel, "turn_in", [VMEM], shape(ZC, 1, 128))(got)
-    got = lax.all_to_all(to_send, ("z", "c"), 0, 0, tiled=True)
+    got = lax.all_to_all(to_send, ("c", "z"), 0, 0, tiled=True)
     rows, to_send = call(
         grid_kernel, "grid", [VMEM] * 5, [shape(2, NA_PAD, NB), shape(ZC, 1, 128)]
     )(got, factor, outer, cosine, sine)
-    got = lax.all_to_all(to_send, ("z", "c"), 0, 0, tiled=True)
+    got = lax.all_to_all(to_send, ("c", "z"), 0, 0, tiled=True)
     to_send = call(turn_out_kernel, "turn_out", [VMEM], shape(YX, 1, 128))(got)
     got = lax.all_to_all(to_send, ("x", "y"), 0, 0, tiled=True)
     spectral_out, grid_field = call(

time: 74.9 us -> 74.8 us (level)
  no operation moved by 1% of the time
where the time goes in v7:
time: 74.8 us; the launch traced here: 74.5 us
  blocking collectives  69.8 us (93%)
  Pallas kernels  3.08 us (4%)
  local copies, waits for them, and re-layouts  0.9 us (1%)
    all_to_all x2, blocking collectives, shards(): got = lax.all_to_all(to_send, ('c', 'z'), 0, 0, tiled=True)  39.3 us
    all_to_all x2, blocking collectives, shards(): got = lax.all_to_all(to_send, ('x', 'y'), 0, 0, tiled=True)  30.5 us

profile of v7, /device:TPU:1, one launch (start us, length us, event | category | flops | bytes accessed | tf_op | source)
XLA Modules:
  0.0 74.5 jit_solution(8418657146632494306)
XLA Ops:
  0.6 0.0 copy-start
  0.6 0.0 copy-start.1
  0.6 0.0 copy-start.2
  0.7 0.1 select.1
  0.8 0.0 copy-start.3
  0.8 0.0 copy-start.4
  0.8 0.9 %copy-done = bf16[1,1,640,384]{3,2,1,0:T(8,128)(2,1)S(1)} copy-done((bf16[1,1,640,384]{3,2,1,0:T(8,128)(2,1)S(1)}, bf16[1,1,640,384]{3,2,1,0:T(8,128)(2,1)}, u32[]{:S(2)}) %copy-start) | copy-done | bytes 491544
  1.7 0.0 copy-done.1
  1.7 0.0 copy-done.2
  1.7 0.0 copy-done.3
  1.7 0.0 copy-done.4
  1.7 0.7 start.1
  2.4 18.9 %all_to_all.20.got_ref = f32[32,1,128]{2,1,0:T(1,128)S(1)} all-to-all(f32[32,1,128]{2,1,0:T(1,128)S(1)} %get-tuple-element.19), channel_id=1, replica_groups=mesh['z'=12,'y'=8,'c'=2,'x'=4] {'x','y'}, dimensions={0} | all-to-all | bytes 32768 | tf_op jit(solution)/shard_map/all_to_all | solution.py:301
  21.4 0.1 turn_in.1
  21.5 26.4 %all_to_all.21.got_ref = f32[24,1,128]{2,1,0:T(1,128)S(1)} all-to-all(f32[24,1,128]{2,1,0:T(1,128)S(1)} %turn_in.1), channel_id=1, replica_groups=mesh['z'=12,'y'=8,'c'=2,'x'=4] {'c','z'}, dimensions={0} | all-to-all | bytes 24576 | tf_op jit(solution)/shard_map/all_to_all | solution.py:303
  47.9 1.0 %grid.1 = (f32[2,24,128]{2,1,0:T(8,128)S(1)}, f32[24,1,128]{2,1,0:T(1,128)S(1)}) custom-call(f32[24,1,128]{2,1,0:T(1,128)S(1)} %all_to_all.21.got_ref, f32[8,768]{1,0:T(8,128)S(1)} %get-tuple-element.20.factor_ref, bf16[2,48,1536]{2,1,0:T(8,128)(2,1)S(1)} %get-tuple-element.21.outer_ref, f32[2,24,768]{2,1,0:T(8,128)S(1)} %get-tuple-element.22.cos_ref, ...), custom_call_target="tpu_custom_call" | custom-call | flops 1000000 | bytes 100000 | tf_op jit(solution)/shard_map/grid/pallas_call | solution.py:304
  48.9 12.8 %all_to_all.22.got_ref = f32[24,1,128]{2,1,0:T(1,128)S(1)} all-to-all(f32[24,1,128]{2,1,0:T(1,128)S(1)} %get-tuple-element.24), channel_id=1, replica_groups=mesh['z'=12,'y'=8,'c'=2,'x'=4] {'c','z'}, dimensions={0} | all-to-all | bytes 24576 | tf_op jit(solution)/shard_map/all_to_all | solution.py:307
  61.8 0.1 turn_out.1
  61.9 11.6 %all_to_all.23.got_ref = f32[32,1,128]{2,1,0:T(1,128)S(1)} all-to-all(f32[32,1,128]{2,1,0:T(1,128)S(1)} %turn_out.1), channel_id=1, replica_groups=mesh['z'=12,'y'=8,'c'=2,'x'=4] {'x','y'}, dimensions={0} | all-to-all | bytes 32768 | tf_op jit(solution)/shard_map/all_to_all | solution.py:309
  73.5 1.0 %legendre_out.1 = (bf16[1,1,4,1280]{3,2,1,0:T(4,128)(2,1)}, bf16[1,2,2688]{2,1,0:T(2,128)(2,1)}) custom-call(f32[1,128]{1,0:T(1,128)S(1)} %get-tuple-element.17.wave_ref, bf16[384,128]{1,0:T(8,128)(2,1)S(1)} %get-tuple-element.16.select_ref, f32[1,384]{1,0:T(1,128)S(1)} %get-tuple-element.18.weight_ref, f32[32,1,128]{2,1,0:T(1,128)S(1)} %all_to_all.23.got_ref, ...), custom_call_target="tpu_custom_call" | custom-call | flops 1000000 | bytes 100000 | tf_op jit(solution)/shard_map/legendre_out/pallas_call | solution.py:310
Async XLA Ops:
  0.6 1.0 %copy-start = (bf16[1,1,640,384]{3,2,1,0:T(8,128)(2,1)S(1)}, bf16[1,1,640,384]{3,2,1,0:T(8,128)(2,1)}, u32[]{:S(2)}) copy-start(bf16[1,1,640,384]{3,2,1,0:T(8,128)(2,1)} %leg_ref.3) | copy-start | bytes 1474564
  0.6 1.0 %copy-start.1 = (bf16[1,1,4,1280]{3,2,1,0:T(4,128)(2,1)S(1)}, bf16[1,1,4,1280]{3,2,1,0:T(4,128)(2,1)}, u32[]{:S(2)}) copy-start(bf16[1,1,4,1280]{3,2,1,0:T(4,128)(2,1)} %spec_ref.1) | copy-start | bytes 30724
  0.6 1.0 %copy-start.2 = (s32[4,192]{1,0:T(4,128)S(1)}, s32[4,192]{1,0:T(4,128)}, u32[]{:S(2)}) copy-start(s32[4,192]{1,0:T(4,128)} %waves_ref.1) | copy-start | bytes 9220
  0.8 0.9 %copy-start.3 = (f32[384]{0:T(512)S(1)}, f32[384]{0:T(512)}, u32[]{:S(2)}) copy-start(f32[384]{0:T(512)} %weight_ref.1) | copy-start | bytes 4612
  0.8 0.9 %copy-start.4 = (s32[2]{0:T(128)S(1)}, s32[2]{0:T(128)}, u32[]{:S(2)}) copy-start(s32[2]{0:T(128)} %length_ref.1) | copy-start | bytes 28

commit v8 on v7

--- a/solution.py
+++ b/solution.py
@@ -18,7 +18,7 @@
 NB = 128
 NA = 21
 NA_PAD = 24
-NT = 48
+NT = 24
 
 PARTS = [slice(q * 128, (q + 1) * 128) for q in range(6)]
 
@@ -143,8 +143,7 @@
     parts = []
     for lanes in PARTS:
         parts += [cosine[:NA_PAD, lanes], sine[:NA_PAD, lanes]]
-    high, low = split(jnp.concatenate(parts, 1))
-    outer = jnp.concatenate([high.astype(F32), low.astype(F32)], 0).astype(BF16)
+    outer = jnp.concatenate(parts, 1).astype(BF16)
     return outer, cosine[NA_PAD:], sine[NA_PAD:]
 
 
@@ -156,9 +155,8 @@
     return jnp.concatenate(rows + [jnp.zeros((3, SLOTS), F32)], 0)
 
 
-def grid_rows(got, factor, outer, cosine, sine):
+def grid_rows(got, factor, outer, cosine, sine, mix_ref):
     got = swap_fours(got)
-    raws = [jnp.zeros((NB, NT), F32) for _ in range(2)]
     for q, lanes in enumerate(PARTS):
         for r in range(2):
             wide = slice(q * 256, (q + 1) * 256)
@@ -173,18 +171,16 @@
                 mixed.append(
                     jnp.concatenate([start_real * c - start_imag * s, -(start_real * s + start_imag * c)], 1)
                 )
-            high = jnp.concatenate(mixed, 0).astype(BF16)
-            raws[r] = raws[r] + dot(high, outer[r, :, wide], ((1,), (1,)))
+            mix_ref[r, :, wide] = jnp.concatenate(mixed, 0).astype(BF16)
     grids, flips = [], []
     for r in range(2):
-        raw = raws[r].T
-        raw = raw[:NA_PAD] + raw[NA_PAD:]
+        raw = dot(outer[r], mix_ref[r], ((1,), (1,)))
         shaped = raw * (1.0 + 0.5 * jnp.tanh(raw))
         point = iota((NA_PAD, NB), 0) * NB + iota((NA_PAD, NB), 1)
         shaped = jnp.where(point.astype(F32) < factor[3 + r : 4 + r, :NB], shaped, 0.0)
         rounded = shaped.astype(BF16).astype(F32)
         grids.append(rounded)
-        flips.append(jnp.concatenate([rounded, rounded], 0).T.astype(BF16))
+        flips.append(rounded.T.astype(BF16))
     lines = [None] * 24
     for q, lanes in enumerate(PARTS):
         for r in range(2):
@@ -236,9 +232,9 @@
     out_ref[...] = turn(got_ref[...].reshape(YX, 128))[:ZC].reshape(ZC, 1, 128)
 
 
-def grid_kernel(got_ref, factor_ref, outer_ref, cos_ref, sin_ref, rows_ref, out_ref):
+def grid_kernel(got_ref, factor_ref, outer_ref, cos_ref, sin_ref, rows_ref, out_ref, mix_ref):
     one, two, out = grid_rows(
-        got_ref[...].reshape(ZC, 128), factor_ref, outer_ref, cos_ref, sin_ref
+        got_ref[...].reshape(ZC, 128), factor_ref, outer_ref, cos_ref, sin_ref, mix_ref
     )
     rows_ref[0] = one
     rows_ref[1] = two
@@ -251,19 +247,19 @@
 
 
 def legendre_out_kernel(wave_ref, select_ref, weight_ref, got_ref, leg_ref, rows_ref, out_ref, grid_ref):
-    for a in range(NA):
-        grid_ref[0, :, a * NB : (a + 1) * NB] = rows_ref[:, a, :].astype(BF16)
     wave = wave_ref[:, :1].astype(jnp.int32)
     real, imag = legendre_out(got_ref[...].reshape(YX, 128), weight_ref[...], leg_ref[0, 0], wave, select_ref[...])
     out_ref[0, 0, :, :NDEG] = real.astype(BF16)
     out_ref[0, 0, :, NDEG:] = imag.astype(BF16)
+    for a in range(NA):
+        grid_ref[0, :, a * NB : (a + 1) * NB] = rows_ref[:, a, :].astype(BF16)
 
 
 VMEM = pl.BlockSpec(memory_space=pltpu.VMEM)
 SMEM = pl.BlockSpec(memory_space=pltpu.SMEM)
 
 
-def call(kernel, name, in_specs, outs, flops=10**6):
+def call(kernel, name, in_specs, outs, flops=10**6, scratch=()):
     single = not isinstance(outs, list)
     return pl.pallas_call(
         kernel,
@@ -271,6 +267,7 @@
         in_specs=in_specs,
         out_specs=VMEM if single else [VMEM] * len(outs),
         out_shape=outs if single else tuple(outs),
+        scratch_shapes=scratch,
         compiler_params=pltpu.CompilerParams(vmem_limit_bytes=24 * 1024 * 1024),
         cost_estimate=pl.CostEstimate(flops=flops, bytes_accessed=100000, transcendentals=0),
     )
@@ -293,7 +290,7 @@
             shape(1, 128),
             shape(1, NLAT),
             shape(8, SLOTS),
-            shape(2, 2 * NA_PAD, 2 * SLOTS, dtype=BF16),
+            shape(2, NT, 2 * SLOTS, dtype=BF16),
             shape(2, 24, SLOTS),
             shape(2, 24, SLOTS),
         ],
@@ -302,7 +299,11 @@
     to_send = call(turn_in_kernel, "turn_in", [VMEM], shape(ZC, 1, 128))(got)
     got = lax.all_to_all(to_send, ("c", "z"), 0, 0, tiled=True)
     rows, to_send = call(
-        grid_kernel, "grid", [VMEM] * 5, [shape(2, NA_PAD, NB), shape(ZC, 1, 128)]
+        grid_kernel,
+        "grid",
+        [VMEM] * 5,
+        [shape(2, NA_PAD, NB), shape(ZC, 1, 128)],
+        scratch=[pltpu.VMEM((2, NB, 2 * SLOTS), BF16)],
     )(got, factor, outer, cosine, sine)
     got = lax.all_to_all(to_send, ("c", "z"), 0, 0, tiled=True)
     to_send = call(turn_out_kernel, "turn_out", [VMEM], shape(YX, 1, 128))(got)

time: 74.8 us -> 74.7 us (level)
  no operation moved by 1% of the time
where the time goes in v8:
time: 74.7 us; the launch traced here: 74.5 us
  blocking collectives  69.8 us (93%)
  Pallas kernels  3.04 us (4%)
  local copies, waits for them, and re-layouts  0.9 us (1%)
    all_to_all x2, blocking collectives, shards(): got = lax.all_to_all(to_send, ('c', 'z'), 0, 0, tiled=True)  39.3 us
    all_to_all x2, blocking collectives, shards(): got = lax.all_to_all(to_send, ('x', 'y'), 0, 0, tiled=True)  30.6 us

profile of v8, /device:TPU:1, one launch (start us, length us, event | category | flops | bytes accessed | tf_op | source)
XLA Modules:
  0.0 74.5 jit_solution(2390518151684918496)
XLA Ops:
  0.6 0.0 copy-start
  0.6 0.0 copy-start.1
  0.6 0.0 copy-start.2
  0.7 0.1 select.1
  0.8 0.0 copy-start.3
  0.8 0.0 copy-start.4
  0.8 0.9 %copy-done = bf16[1,1,640,384]{3,2,1,0:T(8,128)(2,1)S(1)} copy-done((bf16[1,1,640,384]{3,2,1,0:T(8,128)(2,1)S(1)}, bf16[1,1,640,384]{3,2,1,0:T(8,128)(2,1)}, u32[]{:S(2)}) %copy-start) | copy-done | bytes 491544
  1.7 0.0 copy-done.1
  1.7 0.0 copy-done.2
  1.7 0.0 copy-done.3
  1.7 0.0 copy-done.4
  1.7 0.7 start.1
  2.4 18.9 %all_to_all.20.got_ref = f32[32,1,128]{2,1,0:T(1,128)S(1)} all-to-all(f32[32,1,128]{2,1,0:T(1,128)S(1)} %get-tuple-element.19), channel_id=1, replica_groups=mesh['z'=12,'y'=8,'c'=2,'x'=4] {'x','y'}, dimensions={0} | all-to-all | bytes 32768 | tf_op jit(solution)/shard_map/all_to_all | solution.py:298
  21.4 0.1 turn_in.1
  21.5 26.4 %all_to_all.21.got_ref = f32[24,1,128]{2,1,0:T(1,128)S(1)} all-to-all(f32[24,1,128]{2,1,0:T(1,128)S(1)} %turn_in.1), channel_id=1, replica_groups=mesh['z'=12,'y'=8,'c'=2,'x'=4] {'c','z'}, dimensions={0} | all-to-all | bytes 24576 | tf_op jit(solution)/shard_map/all_to_all | solution.py:300
  47.9 1.0 %grid.1 = (f32[2,24,128]{2,1,0:T(8,128)S(1)}, f32[24,1,128]{2,1,0:T(1,128)S(1)}) custom-call(f32[24,1,128]{2,1,0:T(1,128)S(1)} %all_to_all.21.got_ref, f32[8,768]{1,0:T(8,128)S(1)} %get-tuple-element.20.factor_ref, bf16[2,24,1536]{2,1,0:T(8,128)(2,1)S(1)} %get-tuple-element.21.outer_ref, f32[2,24,768]{2,1,0:T(8,128)S(1)} %get-tuple-element.22.cos_ref, ...), custom_call_target="tpu_custom_call" | custom-call | flops 1000000 | bytes 100000 | tf_op jit(solution)/shard_map/grid/pallas_call | solution.py:301
  48.9 12.8 %all_to_all.22.got_ref = f32[24,1,128]{2,1,0:T(1,128)S(1)} all-to-all(f32[24,1,128]{2,1,0:T(1,128)S(1)} %get-tuple-element.24), channel_id=1, replica_groups=mesh['z'=12,'y'=8,'c'=2,'x'=4] {'c','z'}, dimensions={0} | all-to-all | bytes 24576 | tf_op jit(solution)/shard_map/all_to_all | solution.py:308
  61.7 0.1 turn_out.1
  61.9 11.6 %all_to_all.23.got_ref = f32[32,1,128]{2,1,0:T(1,128)S(1)} all-to-all(f32[32,1,128]{2,1,0:T(1,128)S(1)} %turn_out.1), channel_id=1, replica_groups=mesh['z'=12,'y'=8,'c'=2,'x'=4] {'x','y'}, dimensions={0} | all-to-all | bytes 32768 | tf_op jit(solution)/shard_map/all_to_all | solution.py:310
  73.5 1.0 %legendre_out.1 = (bf16[1,1,4,1280]{3,2,1,0:T(4,128)(2,1)}, bf16[1,2,2688]{2,1,0:T(2,128)(2,1)}) custom-call(f32[1,128]{1,0:T(1,128)S(1)} %get-tuple-element.17.wave_ref, bf16[384,128]{1,0:T(8,128)(2,1)S(1)} %get-tuple-element.16.select_ref, f32[1,384]{1,0:T(1,128)S(1)} %get-tuple-element.18.weight_ref, f32[32,1,128]{2,1,0:T(1,128)S(1)} %all_to_all.23.got_ref, ...), custom_call_target="tpu_custom_call" | custom-call | flops 1000000 | bytes 100000 | tf_op jit(solution)/shard_map/legendre_out/pallas_call | solution.py:311
Async XLA Ops:
  0.6 1.0 %copy-start = (bf16[1,1,640,384]{3,2,1,0:T(8,128)(2,1)S(1)}, bf16[1,1,640,384]{3,2,1,0:T(8,128)(2,1)}, u32[]{:S(2)}) copy-start(bf16[1,1,640,384]{3,2,1,0:T(8,128)(2,1)} %leg_ref.3) | copy-start | bytes 1474564
  0.6 1.0 %copy-start.1 = (bf16[1,1,4,1280]{3,2,1,0:T(4,128)(2,1)S(1)}, bf16[1,1,4,1280]{3,2,1,0:T(4,128)(2,1)}, u32[]{:S(2)}) copy-start(bf16[1,1,4,1280]{3,2,1,0:T(4,128)(2,1)} %spec_ref.1) | copy-start | bytes 30724
  0.6 1.0 %copy-start.2 = (s32[4,192]{1,0:T(4,128)S(1)}, s32[4,192]{1,0:T(4,128)}, u32[]{:S(2)}) copy-start(s32[4,192]{1,0:T(4,128)} %waves_ref.1) | copy-start | bytes 9220
  0.8 0.9 %copy-start.3 = (f32[384]{0:T(512)S(1)}, f32[384]{0:T(512)}, u32[]{:S(2)}) copy-start(f32[384]{0:T(512)} %weight_ref.1) | copy-start | bytes 4612
  0.8 0.9 %copy-start.4 = (s32[2]{0:T(128)S(1)}, s32[2]{0:T(128)}, u32[]{:S(2)}) copy-start(s32[2]{0:T(128)} %length_ref.1) | copy-start | bytes 28
